TPU v7x, 32 devices: a whole 2x2x4 slice. The times are simulated.
32 devices in a mesh: ctx: 16 (over z, y, x), wsh: 2 (over core).
Axes of the slice: x: 2, y: 2, z: 4, core: 2. Of those that a mesh axis runs over, the one named last changes fastest.
Arguments:
- tokens_in: bfloat16 [8192, 1088], P(('ctx', 'wsh')), may hold values from -6 to 6
- doc_lengths: int32 [8], replicated, may hold values from 1 to 4096, 8192 in all
- doc_adapter: int32 [8], replicated, may hold values from 0 to 7
- norm1_gain: bfloat16 [1088], P('wsh'), may hold values from 0.5 to 1.5
- norm1_bias: bfloat16 [1088], P('wsh'), may hold values from -1.75 to 1.75
- norm2_gain: bfloat16 [1088], P('wsh'), may hold values from 0.5 to 1.5
- norm2_bias: bfloat16 [1088], P('wsh'), may hold values from -1.75 to 1.75
- w_query: bfloat16 [1088, 1088], P('wsh'), may hold values from -0.1875 to 0.1875
- w_key: bfloat16 [1088, 1088], P('wsh'), may hold values from -0.1875 to 0.1875
- w_value: bfloat16 [1088, 1088], P('wsh'), may hold values from -0.1875 to 0.1875
- w_out: bfloat16 [1088, 1088], P('wsh'), may hold values from -0.75 to 0.75
- w_up: bfloat16 [1088, 4352], P('wsh'), may hold values from -0.1875 to 0.1875
- w_down: bfloat16 [4352, 1088], P(None, 'wsh'), may hold values from -0.09375 to 0.09375
- a_query: bfloat16 [1088, 128], replicated, may hold values from -0.1875 to 0.1875
- b_query: bfloat16 [128, 1088], replicated, may hold values from -1.5 to 1.5
- a_key: bfloat16 [1088, 128], replicated, may hold values from -0.1875 to 0.1875
- b_key: bfloat16 [128, 1088], replicated, may hold values from -1.5 to 1.5
- a_value: bfloat16 [1088, 128], replicated, may hold values from -0.1875 to 0.1875
- b_value: bfloat16 [128, 1088], replicated, may hold values from -1.5 to 1.5
- a_out: bfloat16 [1088, 128], replicated, may hold values from -0.75 to 0.75
- b_out: bfloat16 [128, 1088], replicated, may hold values from -1.5 to 1.5
- a_up: bfloat16 [1088, 128], replicated, may hold values from -0.1875 to 0.1875
- b_up: bfloat16 [128, 4352], replicated, may hold values from -1.5 to 1.5
- a_down: bfloat16 [4352, 128], replicated, may hold values from -0.09375 to 0.09375
- b_down: bfloat16 [128, 1088], replicated, may hold values from -1.5 to 1.5
- cotangent: bfloat16 [8192, 1088], P(('ctx', 'wsh')), may hold values from -6 to 6
Outputs:
- output: bfloat16 [8192, 1088], P(('ctx', 'wsh'))
- grad_in: bfloat16 [8192, 1088], P(('ctx', 'wsh'))
- grad_a_query: float32 [1088, 128], replicated
- grad_b_query: float32 [128, 1088], replicated
- grad_a_key: float32 [1088, 128], replicated
- grad_b_key: float32 [128, 1088], replicated
- grad_a_value: float32 [1088, 128], replicated
- grad_b_value: float32 [128, 1088], replicated
- grad_a_out: float32 [1088, 128], replicated
- grad_b_out: float32 [128, 1088], replicated
- grad_a_up: float32 [1088, 128], replicated
- grad_b_up: float32 [128, 4352], replicated
- grad_a_down: float32 [4352, 128], replicated
- grad_b_down: float32 [128, 1088], replicated
Inputs may be any that keep to these rules, and one draw needn't show every extreme that they name: `doc_lengths`: the documents lie end to end in the stream and fill it; the longest has exactly 4096 tokens.
All inputs are finite; a program needn't handle non-finite values.
Results may differ from a plain program's by a relative error of at most 0.019.
Values may be sent and summed in bfloat16 or wider, within the bound.
No kernel may reach another device: no remote copies, remote signals or barrier semaphores. Data moves between devices by JAX's collectives and lax.ppermute only.
A program may use at most 320 MiB of HBM per device.

v0:
```python
import jax
import jax.numpy as jnp
from jax import lax
from jax.sharding import PartitionSpec as P

HEAD = 64
RANK = 16
DOC_MAX = 4096


EPSILON = 1e-05
NEG_FILL = -1e30


def shifted(array, axis, by):
    size = lax.axis_size(axis)
    pairs = [(i, i + by) for i in range(size) if 0 <= i + by < size]
    return lax.ppermute(array, axis, pairs)


def norm_parts(values, gain, shift):
    row_mean = jnp.mean(values, axis=-1, keepdims=True)
    centered = values - row_mean
    variance = jnp.mean(centered * centered, axis=-1, keepdims=True)
    inverse = lax.rsqrt(variance + EPSILON)
    normed = centered * inverse
    return (normed * gain + shift, normed, inverse)


def norm_back(grad, normed, inverse, gain):
    scaled = grad * gain
    return inverse * (
        scaled
        - jnp.mean(scaled, axis=-1, keepdims=True)
        - normed * jnp.mean(scaled * normed, axis=-1, keepdims=True)
    )


def plain_dot(left, right):
    return jnp.dot(left, right, preferred_element_type=jnp.float32)


def left_tdot(left, right):
    return lax.dot_general(
        left, right, (((0,), (0,)), ((), ())), preferred_element_type=jnp.float32
    )


def right_tdot(left, right):
    return lax.dot_general(
        left, right, (((1,), (1,)), ((), ())), preferred_element_type=jnp.float32
    )


def adapted(hidden, weight, down_a, up_b, adapter_mask):
    inner = (adapter_mask * plain_dot(hidden, down_a)).astype(jnp.bfloat16)
    return (plain_dot(hidden, weight) + plain_dot(inner, up_b), inner)


def adapted_back(grad, hidden, weight, down_a, up_b, inner, mask_low):
    inner_grad = right_tdot(grad, up_b).astype(jnp.bfloat16) * mask_low
    hidden_grad = right_tdot(grad, weight) + right_tdot(inner_grad, down_a)
    return (hidden_grad, left_tdot(hidden, inner_grad), left_tdot(inner, grad))


def document_of(positions, doc_ends):
    inside = jnp.sum((doc_ends[None, :] <= positions[:, None]).astype(jnp.int32), axis=1)
    return jnp.where(positions < 0, -1, inside)


def local(
    tokens_in,
    doc_lengths,
    doc_adapter,
    norm1_gain,
    norm1_bias,
    norm2_gain,
    norm2_bias,
    w_query,
    w_key,
    w_value,
    w_out,
    w_up,
    w_down,
    a_query,
    b_query,
    a_key,
    b_key,
    a_value,
    b_value,
    a_out,
    b_out,
    a_up,
    b_up,
    a_down,
    b_down,
    cotangent,
):
    group_size = lax.axis_size("wsh")
    cycle_size = lax.axis_size("ctx")
    tok_dev = tokens_in.shape[0]
    width_all = tokens_in.shape[1]
    head_count = width_all // HEAD
    block_len = tok_dev * group_size
    hop_count = (DOC_MAX + block_len - 2) // block_len
    cycle_pos = lax.axis_index("ctx")
    first_row = cycle_pos * block_len + lax.axis_index("wsh") * tok_dev
    doc_ends = jnp.cumsum(doc_lengths)
    query_pos = first_row + jnp.arange(tok_dev, dtype=jnp.int32)
    query_docs = document_of(query_pos, doc_ends)
    doc_numbers = jnp.arange(doc_lengths.shape[0], dtype=jnp.int32)
    token_adapter = jnp.sum(
        jnp.where(query_docs[:, None] == doc_numbers[None, :], doc_adapter[None, :], 0), axis=1
    )
    columns = jnp.arange(a_query.shape[1], dtype=jnp.int32) // RANK
    adapter_mask = (token_adapter[:, None] == columns[None, :]).astype(jnp.float32)
    mask_low = adapter_mask.astype(jnp.bfloat16)
    full = (
        lax.all_gather(w_query, "wsh", axis=0, tiled=True),
        lax.all_gather(w_key, "wsh", axis=0, tiled=True),
        lax.all_gather(w_value, "wsh", axis=0, tiled=True),
        lax.all_gather(w_out, "wsh", axis=0, tiled=True),
        lax.all_gather(w_up, "wsh", axis=0, tiled=True),
        lax.all_gather(w_down, "wsh", axis=1, tiled=True),
        lax.all_gather(norm1_gain, "wsh", axis=0, tiled=True),
        lax.all_gather(norm1_bias, "wsh", axis=0, tiled=True),
        lax.all_gather(norm2_gain, "wsh", axis=0, tiled=True),
        lax.all_gather(norm2_bias, "wsh", axis=0, tiled=True),
    )
    stream = tokens_in.astype(jnp.float32)
    norm_one, normed_one, inverse_one = norm_parts(
        stream, full[6].astype(jnp.float32), full[7].astype(jnp.float32)
    )
    hidden_one = norm_one.astype(jnp.bfloat16)
    query_full, inner_query = adapted(hidden_one, full[0], a_query, b_query, adapter_mask)
    keys_full, inner_key = adapted(hidden_one, full[1], a_key, b_key, adapter_mask)
    values_full, inner_value = adapted(hidden_one, full[2], a_value, b_value, adapter_mask)
    query_low = query_full.astype(jnp.bfloat16)
    own_pair = (keys_full.astype(jnp.bfloat16), values_full.astype(jnp.bfloat16))
    key_pair = (
        lax.all_gather(own_pair[0], "wsh", axis=0, tiled=True),
        lax.all_gather(own_pair[1], "wsh", axis=0, tiled=True),
    )
    kept_pairs = [key_pair]
    for distance in range(hop_count):
        key_pair = shifted((key_pair[0], key_pair[1]), "ctx", 1)
        kept_pairs.append(key_pair)
    scaling = HEAD ** (-0.5)
    query_heads = query_low.reshape(tok_dev, head_count, HEAD)

    def hop_scores(distance):
        key_heads = kept_pairs[distance][0].reshape(block_len, head_count, HEAD)
        key_pos = (cycle_pos - distance) * block_len + jnp.arange(block_len, dtype=jnp.int32)
        allowed = (document_of(key_pos, doc_ends)[None, :] == query_docs[:, None]) & (
            key_pos[None, :] <= query_pos[:, None]
        )
        raw_scores = (
            jnp.einsum("qhd,khd->hqk", query_heads, key_heads, preferred_element_type=jnp.float32)
            * scaling
        )
        return jnp.where(allowed[None], raw_scores, NEG_FILL)

    for distance in range(hop_count + 1):
        scores = hop_scores(distance)
        local_max = jnp.max(scores, axis=-1, keepdims=True)
        if distance == 0:
            row_max = local_max
            row_sum = jnp.sum(jnp.exp(scores - local_max), axis=-1, keepdims=True)
        else:
            new_max = jnp.maximum(row_max, local_max)
            row_sum = row_sum * jnp.exp(row_max - new_max) + jnp.sum(
                jnp.exp(scores - new_max), axis=-1, keepdims=True
            )
            row_max = new_max

    def hop_probs(distance):
        return jnp.exp(hop_scores(distance) - row_max) / row_sum

    mixed = jnp.zeros((tok_dev, head_count, HEAD), jnp.float32)
    for distance in range(hop_count + 1):
        prob_low = hop_probs(distance).astype(jnp.bfloat16)
        value_heads = kept_pairs[distance][1].reshape(block_len, head_count, HEAD)
        mixed = mixed + jnp.einsum(
            "hqk,khd->qhd", prob_low, value_heads, preferred_element_type=jnp.float32
        )
    mixed_low = mixed.reshape(tok_dev, width_all).astype(jnp.bfloat16)
    branch_out, inner_out = adapted(mixed_low, full[3], a_out, b_out, adapter_mask)
    middle = stream + branch_out
    norm_two, normed_two, inverse_two = norm_parts(
        middle, full[8].astype(jnp.float32), full[9].astype(jnp.float32)
    )
    hidden_two = norm_two.astype(jnp.bfloat16)
    upward, inner_up = adapted(hidden_two, full[4], a_up, b_up, adapter_mask)
    active_full, gelu_pull = jax.vjp(lambda value: jax.nn.gelu(value, approximate=True), upward)
    active = active_full.astype(jnp.bfloat16)
    down_out, inner_down = adapted(active, full[5], a_down, b_down, adapter_mask)
    output = (middle + down_out).astype(jnp.bfloat16)
    back_rows = (
        lax.all_gather(w_query, "wsh", axis=0, tiled=True),
        lax.all_gather(w_key, "wsh", axis=0, tiled=True),
        lax.all_gather(w_value, "wsh", axis=0, tiled=True),
        lax.all_gather(w_out, "wsh", axis=0, tiled=True),
        lax.all_gather(w_up, "wsh", axis=0, tiled=True),
        lax.all_gather(w_down, "wsh", axis=1, tiled=True),
        lax.all_gather(norm1_gain, "wsh", axis=0, tiled=True),
        lax.all_gather(norm1_bias, "wsh", axis=0, tiled=True),
        lax.all_gather(norm2_gain, "wsh", axis=0, tiled=True),
        lax.all_gather(norm2_bias, "wsh", axis=0, tiled=True),
    )
    active_grad, grad_a_down, grad_b_down = adapted_back(
        cotangent, active, back_rows[5], a_down, b_down, inner_down, mask_low
    )
    up_grad = gelu_pull(active_grad)[0].astype(jnp.bfloat16)
    hidden_two_grad, grad_a_up, grad_b_up = adapted_back(
        up_grad, hidden_two, back_rows[4], a_up, b_up, inner_up, mask_low
    )
    middle_grad = cotangent.astype(jnp.float32) + norm_back(
        hidden_two_grad, normed_two, inverse_two, back_rows[8].astype(jnp.float32)
    )
    branch_grad = middle_grad.astype(jnp.bfloat16)
    mixed_grad, grad_a_out, grad_b_out = adapted_back(
        branch_grad, mixed_low, back_rows[3], a_out, b_out, inner_out, mask_low
    )
    grad_heads = mixed_grad.astype(jnp.bfloat16).reshape(tok_dev, head_count, HEAD)
    row_delta = jnp.einsum("qhd,qhd->hq", grad_heads.astype(jnp.float32), mixed)[..., None]
    query_grad = jnp.zeros((tok_dev, head_count, HEAD), jnp.float32)
    zero_block = jnp.zeros((block_len, head_count, HEAD), jnp.float32)
    returning = (zero_block, zero_block)
    for distance in range(hop_count, -1, -1):
        hop_key_heads = kept_pairs[distance][0].reshape(block_len, head_count, HEAD)
        hop_value_heads = kept_pairs[distance][1].reshape(block_len, head_count, HEAD)
        probs = hop_probs(distance)
        hop_prob_low = probs.astype(jnp.bfloat16)
        prob_grad = jnp.einsum(
            "qhd,khd->hqk", grad_heads, hop_value_heads, preferred_element_type=jnp.float32
        )
        score_grad = (probs * (prob_grad - row_delta)).astype(jnp.bfloat16)
        query_part = (
            jnp.einsum(
                "hqk,khd->qhd", score_grad, hop_key_heads, preferred_element_type=jnp.float32
            )
            * scaling
        )
        key_part = (
            jnp.einsum("hqk,qhd->khd", score_grad, query_heads, preferred_element_type=jnp.float32)
            * scaling
        )
        value_part = jnp.einsum(
            "hqk,qhd->khd", hop_prob_low, grad_heads, preferred_element_type=jnp.float32
        )
        query_part, key_part, value_part = (query_part, key_part, value_part)
        query_grad = query_grad + query_part
        returning = (returning[0] + key_part, returning[1] + value_part)
        if distance > 0:
            returning = (
                shifted(returning[0].astype(jnp.bfloat16), "ctx", -1).astype(jnp.float32),
                shifted(returning[1].astype(jnp.bfloat16), "ctx", -1).astype(jnp.float32),
            )
    key_grad, value_grad = (
        lax.psum_scatter(
            returning[0].astype(jnp.bfloat16), "wsh", scatter_dimension=0, tiled=True
        ).astype(jnp.float32),
        lax.psum_scatter(
            returning[1].astype(jnp.bfloat16), "wsh", scatter_dimension=0, tiled=True
        ).astype(jnp.float32),
    )
    query_grad_low = query_grad.reshape(tok_dev, width_all).astype(jnp.bfloat16)
    key_grad_low = key_grad.reshape(tok_dev, width_all).astype(jnp.bfloat16)
    value_grad_low = value_grad.reshape(tok_dev, width_all).astype(jnp.bfloat16)
    from_query, grad_a_query, grad_b_query = adapted_back(
        query_grad_low, hidden_one, back_rows[0], a_query, b_query, inner_query, mask_low
    )
    from_key, grad_a_key, grad_b_key = adapted_back(
        key_grad_low, hidden_one, back_rows[1], a_key, b_key, inner_key, mask_low
    )
    from_value, grad_a_value, grad_b_value = adapted_back(
        value_grad_low, hidden_one, back_rows[2], a_value, b_value, inner_value, mask_low
    )
    hidden_one_grad = from_query + from_key + from_value
    stream_grad = middle_grad + norm_back(
        hidden_one_grad, normed_one, inverse_one, back_rows[6].astype(jnp.float32)
    )
    grad_in = stream_grad.astype(jnp.bfloat16)
    summed = lax.psum(
        (
            grad_a_query,
            grad_b_query,
            grad_a_key,
            grad_b_key,
            grad_a_value,
            grad_b_value,
            grad_a_out,
            grad_b_out,
            grad_a_up,
            grad_b_up,
            grad_a_down,
            grad_b_down,
        ),
        ("ctx", "wsh"),
    )
    norm_factor = (tok_dev * group_size * cycle_size) ** (-0.5)
    return (
        output,
        grad_in,
        summed[0] * norm_factor,
        summed[1] * norm_factor,
        summed[2] * norm_factor,
        summed[3] * norm_factor,
        summed[4] * norm_factor,
        summed[5] * norm_factor,
        summed[6] * norm_factor,
        summed[7] * norm_factor,
        summed[8] * norm_factor,
        summed[9] * norm_factor,
        summed[10] * norm_factor,
        summed[11] * norm_factor,
    )


def solution(mesh):
    return jax.shard_map(
        local,
        mesh=mesh,
        in_specs=(
            P(("ctx", "wsh"), None),
            P(),
            P(),
            P("wsh"),
            P("wsh"),
            P("wsh"),
            P("wsh"),
            P("wsh", None),
            P("wsh", None),
            P("wsh", None),
            P("wsh", None),
            P("wsh", None),
            P(None, "wsh"),
            P(),
            P(),
            P(),
            P(),
            P(),
            P(),
            P(),
            P(),
            P(),
            P(),
            P(),
            P(),
            P(("ctx", "wsh"), None),
        ),
        out_specs=(
            P(("ctx", "wsh"), None),
            P(("ctx", "wsh"), None),
            P(),
            P(),
            P(),
            P(),
            P(),
            P(),
            P(),
            P(),
            P(),
            P(),
            P(),
            P(),
        ),
        check_vma=False,
    )
```

profile of v0, /device:TPU:0, one launch (start us, length us, event | category | flops | bytes accessed | tf_op | source)
XLA Modules:
  0.0 1252.9 jit_solution(13713650230636487759)
XLA Ops:
  84.2 18.4 %collective-permute-done.8 = bf16[512,1088]{0,1:T(8,128)(2,1)} collective-permute-done((bf16[512,1088]{0,1:T(8,128)(2,1)}, bf16[512,1088]{0,1:T(8,128)(2,1)}, u32[]{:S(2)}, u32[]{:S(2)}) %collective-permute-start.8) | collective-permute-done | bytes 1114144 | tf_op jit(solution)/shard_map/ppermute | solution.py:18
  107.1 19.3 %collective-permute-done.1 = bf16[512,1088]{0,1:T(8,128)(2,1)} collective-permute-done((bf16[512,1088]{0,1:T(8,128)(2,1)S(1)}, bf16[512,1088]{0,1:T(8,128)(2,1)}, u32[]{:S(2)}, u32[]{:S(2)}) %collective-permute-start.1) | collective-permute-done | bytes 1114144 | tf_op jit(solution)/shard_map/ppermute | solution.py:18
  131.2 19.2 %collective-permute-done.9 = bf16[512,1088]{0,1:T(8,128)(2,1)S(1)} collective-permute-done((bf16[512,1088]{0,1:T(8,128)(2,1)}, bf16[512,1088]{0,1:T(8,128)(2,1)S(1)}, u32[]{:S(2)}, u32[]{:S(2)}) %collective-permute-start.9) | collective-permute-done | bytes 1114144 | tf_op jit(solution)/shard_map/ppermute | solution.py:18
  155.7 18.6 %collective-permute-done.2 = bf16[512,1088]{0,1:T(8,128)(2,1)S(1)} collective-permute-done((bf16[512,1088]{0,1:T(8,128)(2,1)}, bf16[512,1088]{0,1:T(8,128)(2,1)S(1)}, u32[]{:S(2)}, u32[]{:S(2)}) %collective-permute-start.2) | collective-permute-done | bytes 1114144 | tf_op jit(solution)/shard_map/ppermute | solution.py:18
  203.6 18.4 %collective-permute-done.3 = bf16[512,1088]{0,1:T(8,128)(2,1)} collective-permute-done((bf16[512,1088]{0,1:T(8,128)(2,1)S(1)}, bf16[512,1088]{0,1:T(8,128)(2,1)}, u32[]{:S(2)}, u32[]{:S(2)}) %collective-permute-start.3) | collective-permute-done | bytes 1114144 | tf_op jit(solution)/shard_map/ppermute | solution.py:18
  250.4 19.4 %collective-permute-done.4 = bf16[512,1088]{0,1:T(8,128)(2,1)} collective-permute-done((bf16[512,1088]{0,1:T(8,128)(2,1)}, bf16[512,1088]{0,1:T(8,128)(2,1)}, u32[]{:S(2)}, u32[]{:S(2)}) %collective-permute-start.4) | collective-permute-done | bytes 1114144 | tf_op jit(solution)/shard_map/ppermute | solution.py:18
  298.9 18.6 %collective-permute-done.5 = bf16[512,1088]{0,1:T(8,128)(2,1)S(1)} collective-permute-done((bf16[512,1088]{0,1:T(8,128)(2,1)}, bf16[512,1088]{0,1:T(8,128)(2,1)S(1)}, u32[]{:S(2)}, u32[]{:S(2)}) %collective-permute-start.5) | collective-permute-done | bytes 1114144 | tf_op jit(solution)/shard_map/ppermute | solution.py:18
  347.3 17.9 %collective-permute-done.6 = bf16[512,1088]{0,1:T(8,128)(2,1)} collective-permute-done((bf16[512,1088]{0,1:T(8,128)(2,1)S(1)}, bf16[512,1088]{0,1:T(8,128)(2,1)}, u32[]{:S(2)}, u32[]{:S(2)}) %collective-permute-start.6) | collective-permute-done | bytes 1114144 | tf_op jit(solution)/shard_map/ppermute | solution.py:18
  619.4 34.1 %collective-permute-done.16 = bf16[512,17,64]{0,2,1:T(8,128)(2,1)S(1)} collective-permute-done((bf16[512,17,64]{0,2,1:T(8,128)(2,1)S(1)}, bf16[512,17,64]{0,2,1:T(8,128)(2,1)S(1)}, u32[]{:S(2)}, u32[]{:S(2)}) %collective-permute-start.16) | collective-permute-done | bytes 1114144 | tf_op jit(solution)/shard_map/ppermute | solution.py:18
  664.5 17.2 %collective-permute-done.17 = bf16[512,17,64]{0,2,1:T(8,128)(2,1)S(1)} collective-permute-done((bf16[512,17,64]{0,2,1:T(8,128)(2,1)S(1)}, bf16[512,17,64]{0,2,1:T(8,128)(2,1)S(1)}, u32[]{:S(2)}, u32[]{:S(2)}) %collective-permute-start.17) | collective-permute-done | bytes 1114144 | tf_op jit(solution)/shard_map/ppermute | solution.py:18
  692.5 21.3 %collective-permute-done.18 = bf16[512,17,64]{0,2,1:T(8,128)(2,1)} collective-permute-done((bf16[512,17,64]{0,2,1:T(8,128)(2,1)}, bf16[512,17,64]{0,2,1:T(8,128)(2,1)}, u32[]{:S(2)}, u32[]{:S(2)}) %collective-permute-start.18) | collective-permute-done | bytes 1114144 | tf_op jit(solution)/shard_map/ppermute | solution.py:18
  720.6 16.9 %collective-permute-done.25 = bf16[512,17,64]{0,2,1:T(8,128)(2,1)S(1)} collective-permute-done((bf16[512,17,64]{0,2,1:T(8,128)(2,1)}, bf16[512,17,64]{0,2,1:T(8,128)(2,1)S(1)}, u32[]{:S(2)}, u32[]{:S(2)}) %collective-permute-start.25) | collective-permute-done | bytes 1114144 | tf_op jit(solution)/shard_map/ppermute | solution.py:18
  743.1 18.3 %collective-permute-done.19 = bf16[512,17,64]{0,2,1:T(8,128)(2,1)S(1)} collective-permute-done((bf16[512,17,64]{0,2,1:T(8,128)(2,1)S(1)}, bf16[512,17,64]{0,2,1:T(8,128)(2,1)S(1)}, u32[]{:S(2)}, u32[]{:S(2)}) %collective-permute-start.19) | collective-permute-done | bytes 1114144 | tf_op jit(solution)/shard_map/ppermute | solution.py:18
  764.7 20.6 %collective-permute-done.26 = bf16[512,17,64]{0,2,1:T(8,128)(2,1)S(1)} collective-permute-done((bf16[512,17,64]{0,2,1:T(8,128)(2,1)S(1)}, bf16[512,17,64]{0,2,1:T(8,128)(2,1)S(1)}, u32[]{:S(2)}, u32[]{:S(2)}) %collective-permute-start.26) | collective-permute-done | bytes 1114144 | tf_op jit(solution)/shard_map/ppermute | solution.py:18
  791.2 18.0 %collective-permute-done.20 = bf16[512,17,64]{0,2,1:T(8,128)(2,1)S(1)} collective-permute-done((bf16[512,17,64]{0,2,1:T(8,128)(2,1)S(1)}, bf16[512,17,64]{0,2,1:T(8,128)(2,1)S(1)}, u32[]{:S(2)}, u32[]{:S(2)}) %collective-permute-start.20) | collective-permute-done | bytes 1114144 | tf_op jit(solution)/shard_map/ppermute | solution.py:18
  812.8 20.3 %collective-permute-done.27 = bf16[512,17,64]{0,2,1:T(8,128)(2,1)S(1)} collective-permute-done((bf16[512,17,64]{0,2,1:T(8,128)(2,1)S(1)}, bf16[512,17,64]{0,2,1:T(8,128)(2,1)S(1)}, u32[]{:S(2)}, u32[]{:S(2)}) %collective-permute-start.27) | collective-permute-done | bytes 1114144 | tf_op jit(solution)/shard_map/ppermute | solution.py:18
  837.7 19.2 %collective-permute-done.21 = bf16[512,17,64]{0,2,1:T(8,128)(2,1)S(1)} collective-permute-done((bf16[512,17,64]{0,2,1:T(8,128)(2,1)S(1)}, bf16[512,17,64]{0,2,1:T(8,128)(2,1)S(1)}, u32[]{:S(2)}, u32[]{:S(2)}) %collective-permute-start.21) | collective-permute-done | bytes 1114144 | tf_op jit(solution)/shard_map/ppermute | solution.py:18
  860.5 20.4 %collective-permute-done.28 = bf16[512,17,64]{0,2,1:T(8,128)(2,1)} collective-permute-done((bf16[512,17,64]{0,2,1:T(8,128)(2,1)}, bf16[512,17,64]{0,2,1:T(8,128)(2,1)}, u32[]{:S(2)}, u32[]{:S(2)}) %collective-permute-start.28) | collective-permute-done | bytes 1114144 | tf_op jit(solution)/shard_map/ppermute | solution.py:18
  885.9 18.9 %collective-permute-done.22 = bf16[512,17,64]{0,2,1:T(8,128)(2,1)} collective-permute-done((bf16[512,17,64]{0,2,1:T(8,128)(2,1)S(1)}, bf16[512,17,64]{0,2,1:T(8,128)(2,1)}, u32[]{:S(2)}, u32[]{:S(2)}) %collective-permute-start.22) | collective-permute-done | bytes 1114144 | tf_op jit(solution)/shard_map/ppermute | solution.py:18
  908.9 19.7 %collective-permute-done.29 = bf16[512,17,64]{0,2,1:T(8,128)(2,1)S(1)} collective-permute-done((bf16[512,17,64]{0,2,1:T(8,128)(2,1)S(1)}, bf16[512,17,64]{0,2,1:T(8,128)(2,1)S(1)}, u32[]{:S(2)}, u32[]{:S(2)}) %collective-permute-start.29) | collective-permute-done | bytes 1114144 | tf_op jit(solution)/shard_map/ppermute | solution.py:18
  932.4 20.1 %collective-permute-done.23 = bf16[512,17,64]{0,2,1:T(8,128)(2,1)S(1)} collective-permute-done((bf16[512,17,64]{0,2,1:T(8,128)(2,1)S(1)}, bf16[512,17,64]{0,2,1:T(8,128)(2,1)S(1)}, u32[]{:S(2)}, u32[]{:S(2)}) %collective-permute-start.23) | collective-permute-done | bytes 1114144 | tf_op jit(solution)/shard_map/ppermute | solution.py:18
  954.4 18.2 %collective-permute-done.30 = bf16[512,17,64]{0,2,1:T(8,128)(2,1)} collective-permute-done((bf16[512,17,64]{0,2,1:T(8,128)(2,1)S(1)}, bf16[512,17,64]{0,2,1:T(8,128)(2,1)}, u32[]{:S(2)}, u32[]{:S(2)}) %collective-permute-start.30) | collective-permute-done | bytes 1114144 | tf_op jit(solution)/shard_map/ppermute | solution.py:18
  982.0 18.1 %collective-permute-done.31 = bf16[512,17,64]{0,2,1:T(8,128)(2,1)S(1)} collective-permute-done((bf16[512,17,64]{0,2,1:T(8,128)(2,1)S(1)}, bf16[512,17,64]{0,2,1:T(8,128)(2,1)S(1)}, u32[]{:S(2)}, u32[]{:S(2)}) %collective-permute-start.31) | collective-permute-done | bytes 1114144 | tf_op jit(solution)/shard_map/ppermute | solution.py:18
  1038.2 193.1 %all-reduce.8.cloned.1.call-done = (f32[1088,128]{1,0:T(8,128)}, f32[128,1088]{0,1:T(8,128)}, f32[1088,128]{1,0:T(8,128)}, f32[128,1088]{0,1:T(8,128)}, f32[1088...) async-done(((f32[1088,128]{1,0:T(8,128)}, ...) | async-done | bytes 10027024 | tf_op jit(solution)/shard_map/psum | solution.py:284
  (795 shorter events, 590.4 us)
Async XLA Ops:
  41.6 188.4 %all-gather.13.cloned.1.call-start = ((), (), s32[]{:S(2)}) async-start(), calls=%async_computation.4 | async-start | bytes 3760128 | tf_op jit(solution)/shard_map/all_gather | solution.py:119
  42.2 327.6 %all-gather.23.cloned.1.call-start = ((), (), s32[]{:S(2)}) async-start(), calls=%async_computation.9 | async-start | bytes 14204928 | tf_op jit(solution)/shard_map/all_gather | solution.py:124
  42.7 442.6 %all-gather.19.cloned.1.call-start = ((), (), s32[]{:S(2)}) async-start(), calls=%async_computation.7 | async-start | bytes 3760128 | tf_op jit(solution)/shard_map/all_gather | solution.py:122
  43.5 446.6 %all-gather.21.cloned.1.call-start = ((), (), s32[]{:S(2)}) async-start(), calls=%async_computation.8 | async-start | bytes 14204928 | tf_op jit(solution)/shard_map/all_gather | solution.py:123
  78.8 47.6 %collective-permute-start.1 = (bf16[512,1088]{0,1:T(8,128)(2,1)S(1)}, bf16[512,1088]{0,1:T(8,128)(2,1)}, u32[]{:S(2)}, u32[]{:S(2)}) collective-permute-start(bf16[512,1088]{0,1:T(8,128)(2,1)S(1)} %collective-permute-done), channel_id=1, source_target_pairs={{0,2},{2,4},{4,6},{6,8},{8,10},{10,12},{12,14},{14,16},{16,18},{18... | collective-permute-start | bytes 3342344 | tf_op jit(solution)/shard_map/ppermute | solution.py:18
  84.1 928.0 %reduce-scatter.3.cloned.1.call-start = ((), (), s32[]{:S(2)}) async-start(), calls=%async_computation.10 | async-start | bytes 1671168 | tf_op jit(solution)/shard_map/reduce_scatter | solution.py:260
  102.6 47.7 %collective-permute-start.9 = (bf16[512,1088]{0,1:T(8,128)(2,1)}, bf16[512,1088]{0,1:T(8,128)(2,1)S(1)}, u32[]{:S(2)}, u32[]{:S(2)}) collective-permute-start(bf16[512,1088]{0,1:T(8,128)(2,1)} %collective-permute-done.8), channel_id=1, source_target_pairs={{0,2},{2,4},{4,6},{6,8},{8,10},{10,12},{12,14},{14,16},{16,18},{18... | collective-permute-start | bytes 3342344 | tf_op jit(solution)/shard_map/ppermute | solution.py:18
  126.4 47.9 %collective-permute-start.2 = (bf16[512,1088]{0,1:T(8,128)(2,1)}, bf16[512,1088]{0,1:T(8,128)(2,1)S(1)}, u32[]{:S(2)}, u32[]{:S(2)}) collective-permute-start(bf16[512,1088]{0,1:T(8,128)(2,1)} %collective-permute-done.1), channel_id=1, source_target_pairs={{0,2},{2,4},{4,6},{6,8},{8,10},{10,12},{12,14},{14,16},{16,18},{18... | collective-permute-start | bytes 3342344 | tf_op jit(solution)/shard_map/ppermute | solution.py:18
  150.4 47.6 %collective-permute-start.10 = (bf16[512,1088]{0,1:T(8,128)(2,1)S(1)}, bf16[512,1088]{0,1:T(8,128)(2,1)}, u32[]{:S(2)}, u32[]{:S(2)}) collective-permute-start(bf16[512,1088]{0,1:T(8,128)(2,1)S(1)} %collective-permute-done.9), channel_id=1, source_target_pairs={{0,2},{2,4},{4,6},{6,8},{8,10},{10,12},{12,14},{14,16},{16,18},{18... | collective-permute-start | bytes 3342344 | tf_op jit(solution)/shard_map/ppermute | solution.py:18
  174.3 47.6 %collective-permute-start.3 = (bf16[512,1088]{0,1:T(8,128)(2,1)S(1)}, bf16[512,1088]{0,1:T(8,128)(2,1)}, u32[]{:S(2)}, u32[]{:S(2)}) collective-permute-start(bf16[512,1088]{0,1:T(8,128)(2,1)S(1)} %collective-permute-done.2), channel_id=1, source_target_pairs={{0,2},{2,4},{4,6},{6,8},{8,10},{10,12},{12,14},{14,16},{16,18},{18... | collective-permute-start | bytes 3342344 | tf_op jit(solution)/shard_map/ppermute | solution.py:18
  198.0 47.9 %collective-permute-start.11 = (bf16[512,1088]{0,1:T(8,128)(2,1)}, bf16[512,1088]{0,1:T(8,128)(2,1)}, u32[]{:S(2)}, u32[]{:S(2)}) collective-permute-start(bf16[512,1088]{0,1:T(8,128)(2,1)} %collective-permute-done.10), channel_id=1, source_target_pairs={{0,2},{2,4},{4,6},{6,8},{8,10},{10,12},{12,14},{14,16},{16,18},{18... | collective-permute-start | bytes 3342344 | tf_op jit(solution)/shard_map/ppermute | solution.py:18
  221.9 47.9 %collective-permute-start.4 = (bf16[512,1088]{0,1:T(8,128)(2,1)}, bf16[512,1088]{0,1:T(8,128)(2,1)}, u32[]{:S(2)}, u32[]{:S(2)}) collective-permute-start(bf16[512,1088]{0,1:T(8,128)(2,1)} %collective-permute-done.3), channel_id=1, source_target_pairs={{0,2},{2,4},{4,6},{6,8},{8,10},{10,12},{12,14},{14,16},{16,18},{18... | collective-permute-start | bytes 3342344 | tf_op jit(solution)/shard_map/ppermute | solution.py:18
  245.9 47.8 %collective-permute-start.12 = (bf16[512,1088]{0,1:T(8,128)(2,1)}, bf16[512,1088]{0,1:T(8,128)(2,1)S(1)}, u32[]{:S(2)}, u32[]{:S(2)}) collective-permute-start(bf16[512,1088]{0,1:T(8,128)(2,1)} %collective-permute-done.11), channel_id=1, source_target_pairs={{0,2},{2,4},{4,6},{6,8},{8,10},{10,12},{12,14},{14,16},{16,18},{18... | collective-permute-start | bytes 3342344 | tf_op jit(solution)/shard_map/ppermute | solution.py:18
  269.8 47.7 %collective-permute-start.5 = (bf16[512,1088]{0,1:T(8,128)(2,1)}, bf16[512,1088]{0,1:T(8,128)(2,1)S(1)}, u32[]{:S(2)}, u32[]{:S(2)}) collective-permute-start(bf16[512,1088]{0,1:T(8,128)(2,1)} %collective-permute-done.4), channel_id=1, source_target_pairs={{0,2},{2,4},{4,6},{6,8},{8,10},{10,12},{12,14},{14,16},{16,18},{18... | collective-permute-start | bytes 3342344 | tf_op jit(solution)/shard_map/ppermute | solution.py:18
  293.7 49.3 %collective-permute-start.13 = (bf16[512,1088]{0,1:T(8,128)(2,1)S(1)}, bf16[512,1088]{0,1:T(8,128)(2,1)}, u32[]{:S(2)}, u32[]{:S(2)}) collective-permute-start(bf16[512,1088]{0,1:T(8,128)(2,1)S(1)} %collective-permute-done.12), channel_id=1, source_target_pairs={{0,2},{2,4},{4,6},{6,8},{8,10},{10,12},{12,14},{14,16},{16,18},{18... | collective-permute-start | bytes 3342344 | tf_op jit(solution)/shard_map/ppermute | solution.py:18
  317.5 47.6 %collective-permute-start.6 = (bf16[512,1088]{0,1:T(8,128)(2,1)S(1)}, bf16[512,1088]{0,1:T(8,128)(2,1)}, u32[]{:S(2)}, u32[]{:S(2)}) collective-permute-start(bf16[512,1088]{0,1:T(8,128)(2,1)S(1)} %collective-permute-done.5), channel_id=1, source_target_pairs={{0,2},{2,4},{4,6},{6,8},{8,10},{10,12},{12,14},{14,16},{16,18},{18... | collective-permute-start | bytes 3342344 | tf_op jit(solution)/shard_map/ppermute | solution.py:18
  365.2 47.9 %collective-permute-start.7 = (bf16[512,1088]{0,1:T(8,128)(2,1)}, bf16[512,1088]{0,1:T(8,128)(2,1)S(1)}, u32[]{:S(2)}, u32[]{:S(2)}) collective-permute-start(bf16[512,1088]{0,1:T(8,128)(2,1)} %collective-permute-done.6), channel_id=1, source_target_pairs={{0,2},{2,4},{4,6},{6,8},{8,10},{10,12},{12,14},{14,16},{16,18},{18... | collective-permute-start | bytes 3342344 | tf_op jit(solution)/shard_map/ppermute | solution.py:18
  389.2 90.4 %collective-permute-start.15 = (bf16[512,1088]{0,1:T(8,128)(2,1)}, bf16[512,1088]{0,1:T(8,128)(2,1)}, u32[]{:S(2)}, u32[]{:S(2)}) collective-permute-start(bf16[512,1088]{0,1:T(8,128)(2,1)} %collective-permute-done.14), channel_id=1, source_target_pairs={{0,2},{2,4},{4,6},{6,8},{8,10},{10,12},{12,14},{14,16},{16,18},{18... | collective-permute-start | bytes 3342344 | tf_op jit(solution)/shard_map/ppermute | solution.py:18
  601.6 83.0 %collective-permute-start.24 = (bf16[512,17,64]{0,2,1:T(8,128)(2,1)}, bf16[512,17,64]{0,2,1:T(8,128)(2,1)S(1)}, u32[]{:S(2)}, u32[]{:S(2)}) collective-permute-start(bf16[512,17,64]{0,2,1:T(8,128)(2,1)} %fusion.86), channel_id=1, source_target_pairs={{2,0},{4,2},{6,4},{8,6},{10,8},{12,10},{14,12},{16,14},{18,16},{20... | collective-permute-start | bytes 3342344 | tf_op jit(solution)/shard_map/ppermute | solution.py:18
  688.6 49.0 %collective-permute-start.25 = (bf16[512,17,64]{0,2,1:T(8,128)(2,1)}, bf16[512,17,64]{0,2,1:T(8,128)(2,1)S(1)}, u32[]{:S(2)}, u32[]{:S(2)}) collective-permute-start(bf16[512,17,64]{0,2,1:T(8,128)(2,1)} %fusion.36), channel_id=1, source_target_pairs={{2,0},{4,2},{6,4},{8,6},{10,8},{12,10},{14,12},{16,14},{18,16},{20... | collective-permute-start | bytes 3342344 | tf_op jit(solution)/shard_map/ppermute | solution.py:18
  761.8 47.3 %collective-permute-start.20 = (bf16[512,17,64]{0,2,1:T(8,128)(2,1)S(1)}, bf16[512,17,64]{0,2,1:T(8,128)(2,1)S(1)}, u32[]{:S(2)}, u32[]{:S(2)}) collective-permute-start(bf16[512,17,64]{0,2,1:T(8,128)(2,1)S(1)} %fusion.41), channel_id=1, source_target_pairs={{2,0},{4,2},{6,4},{8,6},{10,8},{12,10},{14,12},{16,14},{18,16},{20... | collective-permute-start | bytes 3342344 | tf_op jit(solution)/shard_map/ppermute | solution.py:18
  857.3 47.4 %collective-permute-start.22 = (bf16[512,17,64]{0,2,1:T(8,128)(2,1)S(1)}, bf16[512,17,64]{0,2,1:T(8,128)(2,1)}, u32[]{:S(2)}, u32[]{:S(2)}) collective-permute-start(bf16[512,17,64]{0,2,1:T(8,128)(2,1)S(1)} %fusion.39), channel_id=1, source_target_pairs={{2,0},{4,2},{6,4},{8,6},{10,8},{12,10},{14,12},{16,14},{18,16},{20... | collective-permute-start | bytes 3342344 | tf_op jit(solution)/shard_map/ppermute | solution.py:18
  953.9 61.8 %reduce-scatter.5.cloned.1.call-start = ((), (), s32[]{:S(2)}) async-start(), calls=%async_computation.11 | async-start | bytes 1671168 | tf_op jit(solution)/shard_map/reduce_scatter | solution.py:263
  1001.5 229.8 %all-reduce.8.cloned.1.call-start = ((), (), s32[]{:S(2)}) async-start(), calls=%async_computation.12 | async-start | bytes 20054016 | tf_op jit(solution)/shard_map/psum | solution.py:284
  (271 other events, 5021.9 us)
Sparse Core Ops, SparseCore 0:
  9.7 13.8 all-gather.14
  25.1 12.3 all-gather.8
  39.6 10.2 all-gather.16
  51.9 10.2 all-gather.10
  63.6 12.3 all-gather.12
  77.4 23.0 all-gather.22
  102.0 12.3 all-gather.18
  116.0 23.0 all-gather.20
  954.0 12.5 reduce-scatter.2
  1001.6 13.3 reduce-scatter.4
  1022.6 208.6 all-reduce.7
where the time goes:
time: 1260 us; the launch traced here: 1250 us
  waiting for transfers between devices  742 us (59%)
  matrix products  307 us (24%)
  starting transfers between devices  102 us (8%)
  other arithmetic  67.5 us (5%)
  between operations  18.3 us (1%)
    ppermute x32, waiting for transfers between devices, shifted(): return lax.ppermute(array, axis, pairs)  515 us
    psum x1, waiting for transfers between devices, local(): lax.psum((grad_a_query, grad_b_query, grad_a_key, grad_b_key, grad_a_valu...  193 us
    ppermute x32, starting transfers between devices, shifted(): return lax.ppermute(array, axis, pairs)  102 us
    dot_general x9, matrix products, local(): jnp.einsum('qhd,khd->hqk', grad_heads, hop_value_heads, preferred_element...  56.4 us
    dot_general x9, matrix products, local(): jnp.einsum('hqk,qhd->khd', hop_prob_low, grad_heads, preferred_element_ty...  44.6 us
    dot_general x9, matrix products, hop_scores(): jnp.einsum('qhd,khd->hqk', query_heads, key_heads, preferred_element_type...  41.5 us
    dot_general x9, matrix products, local(): jnp.einsum('hqk,khd->qhd', prob_low, value_heads, preferred_element_type=...  40.8 us
    dot_general x18, matrix products, plain_dot(): return jnp.dot(left, right, preferred_element_type=jnp.float32)  36.8 us
  transfers between devices with their start and end apart: 43, of which 34 were waited for; matrix products, arithmetic and copies ran while one was open for 20% of the time, Pallas kernels for 0%

commit v1 on v0

v1 whole, which is shorter than its diff:
```python
import jax
import jax.numpy as jnp
from jax import lax
from jax.experimental import pallas as pl
from jax.experimental.pallas import tpu as pltpu
from jax.sharding import PartitionSpec as P

HEAD = 64
RANK = 16
DOC_MAX = 4096


EPSILON = 1e-05
NEG_FILL = -1e30
SCALING = HEAD ** (-0.5)
SWAP = [(0, 1), (1, 0)]
VMEM_BYTES = 48 * 1024 * 1024


def norm_parts(values, gain, shift):
    row_mean = jnp.mean(values, axis=-1, keepdims=True)
    centered = values - row_mean
    variance = jnp.mean(centered * centered, axis=-1, keepdims=True)
    inverse = lax.rsqrt(variance + EPSILON)
    normed = centered * inverse
    return (normed * gain + shift, normed, inverse)


def norm_back(grad, normed, inverse, gain):
    scaled = grad * gain
    return inverse * (
        scaled
        - jnp.mean(scaled, axis=-1, keepdims=True)
        - normed * jnp.mean(scaled * normed, axis=-1, keepdims=True)
    )


def dot(left, right, lc=1, rc=0):
    return lax.dot_general(
        left, right, (((lc,), (rc,)), ((), ())), preferred_element_type=jnp.float32
    )


def query_columns(meta_ref, starts_ref, i):
    rows = lax.broadcasted_iota(jnp.int32, (starts_ref.shape[1], 1), 0)
    return starts_ref[i], meta_ref[i, 2] + rows


def masked_scores(query, keys, j, first_key, doc_start, query_pos):
    scores = dot(query, keys)
    key_pos = first_key + j * keys.shape[1] + lax.broadcasted_iota(jnp.int32, (1, keys.shape[1]), 1)
    allowed = (key_pos >= doc_start) & (key_pos <= query_pos)
    return jnp.where(allowed, scores, NEG_FILL)


def forward_kernel(meta_ref, starts_ref, query_ref, pair_ref, low_ref, mixed_ref, lse_ref):
    chunks, _, rows = query_ref.shape

    def chunk(i, carry):
        query = (query_ref[i].astype(jnp.float32) * SCALING).T.astype(jnp.bfloat16)
        doc_start, query_pos = query_columns(meta_ref, starts_ref, i)
        offset = pl.multiple_of(meta_ref[i, 3], 2 * HEAD)

        def block(j, state):
            row_max, row_sum, total = state
            keys = pair_ref[j, pl.ds(offset, HEAD), :]
            values = pair_ref[j, pl.ds(offset + HEAD, HEAD), :]
            scores = masked_scores(query, keys, j, meta_ref[i, 4], doc_start, query_pos)
            new_max = jnp.maximum(row_max, jnp.max(scores, axis=1, keepdims=True))
            probs = jnp.exp(scores - new_max)
            shrink = jnp.exp(row_max - new_max)
            row_sum = row_sum * shrink + jnp.sum(probs, axis=1, keepdims=True)
            total = total * shrink + dot(probs.astype(jnp.bfloat16), values, 1, 1)
            return new_max, row_sum, total

        state = (
            jnp.full((rows, 1), NEG_FILL, jnp.float32),
            jnp.zeros((rows, 1), jnp.float32),
            jnp.zeros((rows, HEAD), jnp.float32),
        )
        row_max, row_sum, total = lax.fori_loop(meta_ref[i, 0], meta_ref[i, 1] + 1, block, state)
        mixed = total / row_sum
        mixed_ref[i] = mixed
        low_ref[i] = mixed.T.astype(jnp.bfloat16)
        lse_ref[i] = row_max + jnp.log(row_sum)
        return carry

    lax.fori_loop(0, chunks, chunk, 0)


def backward_kernel(
    meta_ref, starts_ref, query_ref, pair_ref, grad_ref, mixed_ref, lse_ref, dq_ref, dpair_ref, sum_ref
):
    chunks, _, rows = query_ref.shape
    blocks = pair_ref.shape[0]

    def clear(j, carry):
        sum_ref[j] = jnp.zeros(sum_ref.shape[1:], jnp.float32)
        return carry

    lax.fori_loop(0, blocks, clear, 0)

    def chunk(i, carry):
        query_f = query_ref[i].astype(jnp.float32) * SCALING
        query_t = query_f.astype(jnp.bfloat16)
        query = query_f.T.astype(jnp.bfloat16)
        grad_t = grad_ref[i]
        grad_f = grad_t.astype(jnp.float32).T
        grad = grad_f.astype(jnp.bfloat16)
        delta = jnp.sum(grad_f * mixed_ref[i], axis=1, keepdims=True)
        lse = lse_ref[i]
        doc_start, query_pos = query_columns(meta_ref, starts_ref, i)
        offset = pl.multiple_of(meta_ref[i, 3], 2 * HEAD)

        def block(j, total):
            keys = pair_ref[j, pl.ds(offset, HEAD), :]
            values = pair_ref[j, pl.ds(offset + HEAD, HEAD), :]
            scores = masked_scores(query, keys, j, meta_ref[i, 4], doc_start, query_pos)
            probs = jnp.exp(scores - lse)
            prob_grad = dot(grad, values)
            score_grad = (probs * (prob_grad - delta)).astype(jnp.bfloat16)
            sum_ref[j, pl.ds(offset, HEAD), :] += dot(query_t, score_grad)
            sum_ref[j, pl.ds(offset + HEAD, HEAD), :] += dot(grad_t, probs.astype(jnp.bfloat16))
            return total + dot(score_grad, keys, 1, 1)

        total = lax.fori_loop(
            meta_ref[i, 0], meta_ref[i, 1] + 1, block, jnp.zeros((rows, HEAD), jnp.float32)
        )
        dq_ref[i] = (total * SCALING).T.astype(jnp.bfloat16)
        return carry

    lax.fori_loop(0, chunks, chunk, 0)

    def finish(j, carry):
        dpair_ref[j] = sum_ref[j].astype(jnp.bfloat16)
        return carry

    lax.fori_loop(0, blocks, finish, 0)


SMEM_SPEC = pl.BlockSpec(memory_space=pltpu.SMEM)
VMEM_SPEC = pl.BlockSpec(memory_space=pltpu.VMEM)


def attention_forward(meta, starts, query, pair):
    chunks, _, rows = query.shape
    return pl.pallas_call(
        forward_kernel,
        out_shape=(
            jax.ShapeDtypeStruct(query.shape, jnp.bfloat16),
            jax.ShapeDtypeStruct((chunks, rows, HEAD), jnp.float32),
            jax.ShapeDtypeStruct((chunks, rows, 1), jnp.float32),
        ),
        in_specs=[SMEM_SPEC] + [VMEM_SPEC] * 3,
        out_specs=(VMEM_SPEC,) * 3,
        compiler_params=pltpu.CompilerParams(vmem_limit_bytes=VMEM_BYTES),
        name="attention_forward",
    )(meta, starts, query, pair)


def attention_backward(meta, starts, query, pair, grad, mixed, lse):
    return pl.pallas_call(
        backward_kernel,
        out_shape=(
            jax.ShapeDtypeStruct(query.shape, jnp.bfloat16),
            jax.ShapeDtypeStruct(pair.shape, jnp.bfloat16),
        ),
        in_specs=[SMEM_SPEC] + [VMEM_SPEC] * 6,
        out_specs=(VMEM_SPEC,) * 2,
        scratch_shapes=[pltpu.VMEM(pair.shape, jnp.float32)],
        compiler_params=pltpu.CompilerParams(vmem_limit_bytes=VMEM_BYTES),
        name="attention_backward",
    )(meta, starts, query, pair, grad, mixed, lse)


def summed_rows(packed, cycle_size):
    wide = packed.shape[0]
    bits = cycle_size.bit_length() - 1
    unit = 3 * 2 * cycle_size * 8
    rows = -(-wide // unit) * unit
    packed = jnp.pad(packed, ((0, rows - wide), (0, 0)))
    place, core = lax.axis_index("ctx"), lax.axis_index("wsh")

    def halves(array, bit):
        size = array.shape[0] // 2
        kept = lax.dynamic_slice_in_dim(array, bit * size, size, 0)
        sent = lax.dynamic_slice_in_dim(array, (1 - bit) * size, size, 0)
        return kept, sent

    def joined(own, other, bit):
        size = own.shape[0]
        whole = jnp.concatenate([own, own], axis=0)
        return lax.dynamic_update_slice_in_dim(whole, other, (1 - bit) * size, 0)

    def exchange(array, bit):
        return lax.ppermute(array, "ctx", [(i, i ^ (1 << bit)) for i in range(cycle_size)])

    kept, sent = halves(packed, core)
    mine = kept + lax.ppermute(sent, "wsh", SWAP)
    third = mine.shape[0] // 3
    parts = [mine[i * third : (i + 1) * third] for i in range(3)]
    low = min(3, bits)
    orders = [[(s + i) % low for s in range(low)] + list(range(low, bits)) for i in range(3)]
    for step in range(bits):
        following = []
        for part, order in zip(parts, orders):
            kept, sent = halves(part, (place >> order[step]) & 1)
            following.append(kept + exchange(sent, order[step]))
        parts = following
    for step in reversed(range(bits)):
        parts = [
            joined(part, exchange(part, order[step]), (place >> order[step]) & 1)
            for part, order in zip(parts, orders)
        ]
    mine = jnp.concatenate(parts, axis=0)
    return joined(mine, lax.ppermute(mine, "wsh", SWAP), core)[:wide]


def local(
    tokens_in,
    doc_lengths,
    doc_adapter,
    norm1_gain,
    norm1_bias,
    norm2_gain,
    norm2_bias,
    w_query,
    w_key,
    w_value,
    w_out,
    w_up,
    w_down,
    a_query,
    b_query,
    a_key,
    b_key,
    a_value,
    b_value,
    a_out,
    b_out,
    a_up,
    b_up,
    a_down,
    b_down,
    cotangent,
):
    group_size = lax.axis_size("wsh")
    cycle_size = lax.axis_size("ctx")
    tok_dev, width_all = tokens_in.shape
    head_count = width_all // HEAD
    block_len = tok_dev * group_size
    hop_count = (DOC_MAX + block_len - 2) // block_len
    span = head_count - 1
    cycle_pos = lax.axis_index("ctx")
    core = lax.axis_index("wsh")
    half = width_all // group_size

    first_row = cycle_pos * block_len + core * tok_dev
    doc_ends = jnp.cumsum(doc_lengths)
    doc_starts = doc_ends - doc_lengths
    query_pos = first_row + jnp.arange(tok_dev, dtype=jnp.int32)
    query_docs = jnp.sum((doc_ends[None, :] <= query_pos[:, None]).astype(jnp.int32), axis=1)
    doc_numbers = jnp.arange(doc_lengths.shape[0], dtype=jnp.int32)
    token_adapter = jnp.sum(
        jnp.where(query_docs[:, None] == doc_numbers[None, :], doc_adapter[None, :], 0), axis=1
    )
    columns = jnp.arange(a_query.shape[1], dtype=jnp.int32) // RANK
    adapter_mask = (token_adapter[:, None] == columns[None, :]).astype(jnp.float32)
    mask_low = adapter_mask.astype(jnp.bfloat16)

    team = cycle_pos // span
    past = hop_count if cycle_size > span else 0
    first_key = (team * span - past) * block_len
    chunk_pos = jnp.concatenate(
        [
            (team * span + jnp.arange(span, dtype=jnp.int32)) * block_len + core * tok_dev,
            first_row[None],
        ]
    ).astype(jnp.int32)
    row_pos = chunk_pos[:, None] + jnp.arange(tok_dev, dtype=jnp.int32)[None, :]
    row_starts = jnp.max(
        jnp.where(doc_starts[None, None, :] <= row_pos[:, :, None], doc_starts[None, None, :], 0), axis=2
    )
    meta = jnp.stack(
        [
            (row_starts[:, 0] - first_key) // block_len,
            (chunk_pos - first_key) // block_len,
            chunk_pos,
            jnp.where(jnp.arange(span + 1) == span, 2 * HEAD, 0),
            jnp.full((span + 1,), first_key),
        ],
        axis=1,
    ).astype(jnp.int32)
    starts_col = row_starts[:, :, None].astype(jnp.int32)

    def swap(array):
        return lax.ppermute(array, "wsh", SWAP)

    def ordered(own, other, axis):
        return jnp.where(
            core == 0,
            jnp.concatenate([own, other], axis=axis),
            jnp.concatenate([other, own], axis=axis),
        )

    def own_other(array):
        return (
            lax.dynamic_slice_in_dim(array, core * half, half, 1),
            lax.dynamic_slice_in_dim(array, (1 - core) * half, half, 1),
        )

    if cycle_size > span:
        teams = [[t * span + i for i in range(span)] for t in range(cycle_size // span)]
    else:
        teams = None

    def exchange(blocks):
        return lax.all_to_all(blocks, "ctx", 0, 0, tiled=True, axis_index_groups=teams)

    gains = jnp.stack([norm1_gain, norm1_bias, norm2_gain, norm2_bias])
    gains = ordered(gains, swap(gains), 1).astype(jnp.float32)
    weights = [w_query, w_key, w_value, w_out, w_up, w_down]
    others = [swap(item) for item in weights]

    stream = tokens_in.astype(jnp.float32)
    norm_one, normed_one, inverse_one = norm_parts(stream, gains[0], gains[1])
    hidden_one = norm_one.astype(jnp.bfloat16)
    hidden_own, hidden_other = own_other(hidden_one)

    def projected(number, down_a, up_b):
        inner = (adapter_mask * dot(hidden_one, down_a)).astype(jnp.bfloat16)
        total = (
            dot(weights[number], hidden_own, 0, 1)
            + dot(others[number], hidden_other, 0, 1)
            + dot(up_b, inner, 0, 1)
        )
        return total.astype(jnp.bfloat16).reshape(head_count, HEAD, tok_dev), inner

    query_t, inner_query = projected(0, a_query, b_query)
    keys_t, inner_key = projected(1, a_key, b_key)
    values_t, inner_value = projected(2, a_value, b_value)

    last_pair = jnp.concatenate([keys_t[span:], values_t[span:]], axis=1)
    outgoing = jnp.concatenate(
        [
            query_t[:span],
            keys_t[:span],
            values_t[:span],
            jnp.broadcast_to(last_pair, (span, 2 * HEAD, tok_dev)),
        ],
        axis=1,
    )
    incoming = exchange(outgoing)
    query_all = jnp.concatenate([incoming[:, :HEAD], query_t[span:]], axis=0)
    pair_own = incoming[:, HEAD:]
    pair = ordered(pair_own, swap(pair_own), 2)
    ahead = [(i, i + span) for i in range(cycle_size - span)]
    back = [(i + span, i) for i in range(cycle_size - span)]
    if past:
        pair = jnp.concatenate([lax.ppermute(pair[span - past :], "ctx", ahead), pair], axis=0)

    low_all, mixed_all, lse_all = attention_forward(meta, starts_col, query_all, pair)
    mixed_t = jnp.concatenate([exchange(low_all[:span]), low_all[span:]], axis=0)
    mixed_t = mixed_t.reshape(width_all, tok_dev)
    mixed_low = mixed_t.T

    mixed_own, mixed_other = own_other(mixed_low)
    inner_out = (adapter_mask * dot(mixed_low, a_out)).astype(jnp.bfloat16)
    middle = stream + (
        dot(mixed_own, w_out) + dot(mixed_other, others[3]) + dot(inner_out, b_out)
    )
    norm_two, normed_two, inverse_two = norm_parts(middle, gains[2], gains[3])
    hidden_two = norm_two.astype(jnp.bfloat16)
    two_own, two_other = own_other(hidden_two)
    inner_up = (adapter_mask * dot(hidden_two, a_up)).astype(jnp.bfloat16)
    upward = dot(two_own, w_up) + dot(two_other, others[4]) + dot(inner_up, b_up)
    active_full, gelu_pull = jax.vjp(lambda value: jax.nn.gelu(value, approximate=True), upward)
    active = active_full.astype(jnp.bfloat16)
    inner_down = (adapter_mask * dot(active, a_down)).astype(jnp.bfloat16)
    down_out = ordered(dot(active, w_down), dot(active, others[5]), 1) + dot(inner_down, b_down)
    output = (middle + down_out).astype(jnp.bfloat16)

    def adapter_back(grad, up_b):
        return dot(grad, up_b, 1, 1).astype(jnp.bfloat16) * mask_low

    grad_own, grad_other = own_other(cotangent)
    down_grad = adapter_back(cotangent, b_down)
    active_grad = (
        dot(grad_own, w_down, 1, 1) + dot(grad_other, others[5], 1, 1) + dot(down_grad, a_down, 1, 1)
    )
    up_grad = gelu_pull(active_grad)[0].astype(jnp.bfloat16)
    up_inner_grad = adapter_back(up_grad, b_up)
    hidden_two_grad = ordered(dot(up_grad, w_up, 1, 1), dot(up_grad, others[4], 1, 1), 1) + dot(
        up_inner_grad, a_up, 1, 1
    )
    middle_grad = cotangent.astype(jnp.float32) + norm_back(
        hidden_two_grad, normed_two, inverse_two, gains[2]
    )
    branch_grad = middle_grad.astype(jnp.bfloat16)
    out_inner_grad = adapter_back(branch_grad, b_out)
    mixed_grad_t = ordered(
        dot(w_out, branch_grad, 1, 1), dot(others[3], branch_grad, 1, 1), 0
    ) + dot(a_out, out_inner_grad, 1, 1)
    mixed_grad_t = mixed_grad_t.astype(jnp.bfloat16).reshape(head_count, HEAD, tok_dev)

    grad_all = jnp.concatenate([exchange(mixed_grad_t[:span]), mixed_grad_t[span:]], axis=0)
    dq_all, dpair = attention_backward(
        meta, starts_col, query_all, pair, grad_all, mixed_all, lse_all
    )
    dpair_own = lax.dynamic_slice_in_dim(dpair, core * tok_dev, tok_dev, 2)
    dpair_sent = lax.dynamic_slice_in_dim(dpair, (1 - core) * tok_dev, tok_dev, 2)
    dpair_sum = dpair_own.astype(jnp.float32) + swap(dpair_sent).astype(jnp.float32)
    if past:
        returned = lax.ppermute(dpair_sum[:past].astype(jnp.bfloat16), "ctx", back)
        dpair_sum = dpair_sum[past:]
        dpair_sum = dpair_sum.at[span - past :].add(returned.astype(jnp.float32))
    outgoing_back = jnp.concatenate([dq_all[:span], dpair_sum.astype(jnp.bfloat16)], axis=1)
    incoming_back = exchange(outgoing_back)
    last_sum = jnp.sum(incoming_back[:, 3 * HEAD :].astype(jnp.float32), axis=0).astype(jnp.bfloat16)

    def gathered(first, last):
        main = incoming_back[:, first : first + HEAD].reshape(span * HEAD, tok_dev)
        return jnp.concatenate([main, last], axis=0)

    grads_t = [
        gathered(0, dq_all[span]),
        gathered(HEAD, last_sum[:HEAD]),
        gathered(2 * HEAD, last_sum[HEAD:]),
    ]

    own_sum, other_sum, adapter_sum = 0.0, 0.0, 0.0
    late = []
    for number, (grad_t, down_a, up_b, inner) in enumerate(
        zip(
            grads_t,
            (a_query, a_key, a_value),
            (b_query, b_key, b_value),
            (inner_query, inner_key, inner_value),
        )
    ):
        inner_grad = dot(grad_t, up_b, 0, 1).astype(jnp.bfloat16) * mask_low
        own_sum = own_sum + dot(grad_t, weights[number], 0, 1)
        other_sum = other_sum + dot(grad_t, others[number], 0, 1)
        adapter_sum = adapter_sum + dot(inner_grad, down_a, 1, 1)
        late.append(dot(hidden_one, inner_grad, 0, 0))
        late.append(dot(grad_t, inner, 1, 0))
    hidden_one_grad = ordered(own_sum, other_sum, 1) + adapter_sum
    stream_grad = middle_grad + norm_back(hidden_one_grad, normed_one, inverse_one, gains[0])
    grad_in = stream_grad.astype(jnp.bfloat16)

    norm_factor = (tok_dev * group_size * cycle_size) ** (-0.5)
    early = lax.psum(
        tuple(
            item.astype(jnp.bfloat16)
            for item in (
                dot(mixed_low, out_inner_grad, 0, 0),
                dot(inner_out, branch_grad, 0, 0),
                dot(hidden_two, up_inner_grad, 0, 0),
                dot(inner_up, up_grad, 0, 0),
                dot(active, down_grad, 0, 0),
                dot(inner_down, cotangent, 0, 0),
            )
        ),
        ("ctx", "wsh"),
    )
    early = [item.astype(jnp.float32) * norm_factor for item in early]
    packed = jnp.concatenate([item.astype(jnp.bfloat16) for item in late], axis=0)
    late_sum = summed_rows(packed, cycle_size).astype(jnp.float32) * norm_factor
    late_sum = [late_sum[i * width_all : (i + 1) * width_all] for i in range(6)]
    return (
        output,
        grad_in,
        late_sum[0],
        late_sum[1].T,
        late_sum[2],
        late_sum[3].T,
        late_sum[4],
        late_sum[5].T,
        *early,
    )


def solution(mesh):
    return jax.shard_map(
        local,
        mesh=mesh,
        in_specs=(
            P(("ctx", "wsh"), None),
            P(),
            P(),
            P("wsh"),
            P("wsh"),
            P("wsh"),
            P("wsh"),
            P("wsh", None),
            P("wsh", None),
            P("wsh", None),
            P("wsh", None),
            P("wsh", None),
            P(None, "wsh"),
            P(),
            P(),
            P(),
            P(),
            P(),
            P(),
            P(),
            P(),
            P(),
            P(),
            P(),
            P(),
            P(("ctx", "wsh"), None),
        ),
        out_specs=(
            P(("ctx", "wsh"), None),
            P(("ctx", "wsh"), None),
            P(),
            P(),
            P(),
            P(),
            P(),
            P(),
            P(),
            P(),
            P(),
            P(),
            P(),
            P(),
        ),
        check_vma=False,
    )
```

time: 1260 us -> 574 us (0.46)
  waiting for transfers between devices: 742 us -> 231 us
  matrix products: 307 us -> 84.1 us
  Pallas kernels: 0 us -> 89.9 us
  other arithmetic: 67.5 us -> 32.5 us
  starting transfers between devices: 102 us -> 75.3 us
  local copies, waits for them, and re-layouts: 11.7 us -> 34.8 us
    ppermute x32 -> x35, waiting for transfers between devices: 515 us -> 11.6 us  [the longest x24 9.32 us: exchange(): lax.ppermute(array, 'ctx', [(i, i ^ 1 << bit) for i in range(cycle_size)])]
    dot_general x102 -> x60, matrix products: 307 us -> 84.1 us  [dot(): lax.dot_general(left, right, (((lc,), (rc,)), ((), ())), preferred_elemen...]
    pallas_call x0 -> x2, Pallas kernels: none -> 89.9 us  [the longest x1 48.1 us: attention_backward(): pl.pallas_call(backward_kernel, out_shape=(jax.ShapeDtypeStruct(query.sha...]
    ppermute x32 -> x35, starting transfers between devices: 102 us -> 33.7 us  [the longest x24 31.8 us: exchange(): lax.ppermute(array, 'ctx', [(i, i ^ 1 << bit) for i in range(cycle_size)])]
    all_to_all x0 -> x4, waiting for transfers between devices: none -> 59.4 us  [exchange(): lax.all_to_all(blocks, 'ctx', 0, 0, tiled=True, axis_index_groups=teams)]
    all_to_all x0 -> x4, starting transfers between devices: none -> 41.6 us  [exchange(): lax.all_to_all(blocks, 'ctx', 0, 0, tiled=True, axis_index_groups=teams)]
    psum x1, waiting for transfers between devices: 193 us -> 160 us  [local(): lax.psum(tuple((item.astype(jnp.bfloat16) for item in (dot(mixed_low, out...]
    all_gather x8 -> x0, waiting for transfers between devices: 30.8 us -> none  [the longest x1 9.42 us: local(): lax.all_gather(w_value, 'wsh', axis=0, tiled=True)]
  transfers between devices with their start and end apart: 43 -> 40, of which waited for: 34 -> 19; matrix products, arithmetic and copies ran while one was open for 20% -> 15% of each run, Pallas kernels for 0% -> 7%
where the time goes in v1:
time: 574 us; the launch traced here: 564 us
  waiting for transfers between devices  231 us (40%)
  Pallas kernels  89.9 us (16%)
  matrix products  84.1 us (15%)
  starting transfers between devices  75.3 us (13%)
  local copies, waits for them, and re-layouts  34.8 us (6%)
  other arithmetic  32.5 us (6%)
  between operations  16.2 us (3%)
    psum x1, waiting for transfers between devices, local(): lax.psum(tuple((item.astype(jnp.bfloat16) for item in (dot(mixed_low, out...  160 us
    dot_general x60, matrix products, dot(): lax.dot_general(left, right, (((lc,), (rc,)), ((), ())), preferred_elemen...  84.1 us
    all_to_all x4, waiting for transfers between devices, exchange(): lax.all_to_all(blocks, 'ctx', 0, 0, tiled=True, axis_index_groups=teams)  59.4 us
    pallas_call x1, Pallas kernels, attention_backward(): pl.pallas_call(backward_kernel, out_shape=(jax.ShapeDtypeStruct(query.sha...  48.1 us
    pallas_call x1, Pallas kernels, attention_forward(): pl.pallas_call(forward_kernel, out_shape=(jax.ShapeDtypeStruct(query.shap...  41.8 us
    all_to_all x4, starting transfers between devices, exchange(): lax.all_to_all(blocks, 'ctx', 0, 0, tiled=True, axis_index_groups=teams)  41.6 us
    ppermute x24, starting transfers between devices, exchange(): lax.ppermute(array, 'ctx', [(i, i ^ 1 << bit) for i in range(cycle_size)])  31.8 us
    unnamed x193, local copies, waits for them, and re-layouts  13 us
  transfers between devices with their start and end apart: 40, of which 19 were waited for; matrix products, arithmetic and copies ran while one was open for 15% of the time, Pallas kernels for 7%

profile of v1, /device:TPU:0, one launch (start us, length us, event | category | flops | bytes accessed | tf_op | source)
XLA Modules:
  0.0 563.5 jit_solution(5828698643947266364)
XLA Ops:
  23.5 2.3 convolution_add_fusion.14
  26.1 2.2 convolution_add_fusion.15
  31.6 8.3 %all-to-all-start = ((bf16[16,320,256]{2,1,0:T(8,128)(2,1)}), bf16[16,320,256]{2,1,0:T(8,128)(2,1)}, u32[]{:S(2)}, u32[]{:S(2)}) async-start(bf16[16,320,256]{2,1,0:T(8,128)(2,1)} %pad_maximum_fusion), calls=%async_computation | async-start | bytes 5242880 | tf_op jit(solution)/shard_map/all_to_all | solution.py:318
  40.0 52.0 %all-to-all-done = bf16[16,320,256]{2,1,0:T(8,128)(2,1)} async-done(((bf16[16,320,256]{2,1,0:T(8,128)(2,1)}), bf16[16,320,256]{2,1,0:T(8,128)(2,1)}, u32[]{:S(2)}, u32[]{:S(2)}) %all-to-all-start) | async-done | bytes 2621472 | tf_op jit(solution)/shard_map/all_to_all | solution.py:318
  92.0 3.1 slice.184
  100.0 6.0 %maximum_select_fusion.pair_ref = bf16[16,256,512]{2,1,0:T(8,128)(2,1)} fusion(bf16[16,256,256]{2,1,0:T(8,128)(2,1)} %collective-permute-done.4, bf16[16,256,256]{2,1,0:T(8,128)(2,1)} %slice.184, pred[]{:T(512)S(6)} %eq.45), kind=kLoop, calls=%fused_computation.16 | loop fusion | flops 18874368 | bytes 8388609 | tf_op jit(solution)/shard_map/jit(_where)/select_n | solution.py:300
  106.1 41.8 %attention_forward.1 = (bf16[17,64,256]{2,1,0:T(8,128)(2,1)S(1)}, f32[17,256,64]{2,1,0:T(8,128)S(1)}, f32[17,256,1]{2,1,0:T(8,128)S(1)}) custom-call(s32[17,5]{1,0:T(8,128)S(1)} %stack.22.meta_ref, s32[17,256,1]{2,1,0:T(8,128)} %copy.57.starts_ref, bf16[17,64,256]{2,1,0:T(8,128)(2,1)S(1)} %pad_maximum_fusion.3.query_ref, ...), custom_call_target="tpu_custom_call" | custom-call | tf_op jit(solution)/shard_map/attention_forward/pallas_call | solution.py:147
  151.5 17.1 %all-to-all-start.1 = ((bf16[16,64,256]{2,1,0:T(8,128)(2,1)}), bf16[16,64,256]{2,1,0:T(8,128)(2,1)}, u32[]{:S(2)}, u32[]{:S(2)}) async-start(bf16[16,64,256]{2,1,0:T(8,128)(2,1)} %slice.148), calls=%async_computation.1 | async-start | bytes 1048576 | tf_op jit(solution)/shard_map/all_to_all | solution.py:318
  168.6 4.3 fusion.55
  173.0 6.5 %convolution_add_fusion.2 = f32[256,4352]{1,0:T(8,128)} fusion(f32[256,4352]{1,0:T(8,128)S(1)} %fusion.55, bf16[4352,544]{0,1:T(8,128)(2,1)} %collective-permute-done.7, bf16[256,1088]{0,1:T(8,128)(2,1)S(1)} %copy-done.15, s32[]{:T(128)S(6)} %select_n.198), kind=kOutput, calls=%fused_computation.2 | convolution fusion | flops 1213267968 | bytes 13926404 | tf_op jit(solution)/shard_map/dot_general | solution.py:39
  190.7 4.3 convolution_add_fusion.3
  195.1 3.2 multiply_convert_fusion
  198.3 4.0 fusion.6
  204.6 3.8 fusion.104
  216.1 7.1 %all-to-all-start.2 = ((bf16[16,64,256]{2,1,0:T(8,128)(2,1)}), bf16[16,64,256]{2,1,0:T(8,128)(2,1)}, u32[]{:S(2)}, u32[]{:S(2)}) async-start(bf16[16,64,256]{2,1,0:T(8,128)(2,1)} %bitcast.21), calls=%async_computation.2 | async-start | bytes 1048576 | tf_op jit(solution)/shard_map/all_to_all | solution.py:318
  226.6 7.4 %all-to-all-done.2 = bf16[16,64,256]{2,1,0:T(8,128)(2,1)} async-done(((bf16[16,64,256]{2,1,0:T(8,128)(2,1)}), bf16[16,64,256]{2,1,0:T(8,128)(2,1)}, u32[]{:S(2)}, u32[]{:S(2)}) %all-to-all-start.2) | async-done | bytes 524320 | tf_op jit(solution)/shard_map/all_to_all | solution.py:318
  236.7 48.1 %attention_backward.1 = (bf16[17,64,256]{2,1,0:T(8,128)(2,1)S(1)}, bf16[16,256,512]{2,1,0:T(8,128)(2,1)}) custom-call(s32[17,5]{1,0:T(8,128)S(1)} %stack.22.meta_ref, s32[17,256,1]{2,1,0:T(8,128)S(1)} %copy-done.2, bf16[17,64,256]{2,1,0:T(8,128)(2,1)S(1)} %pad_maximum_fusion.3.query_ref, bf16[16,256,512]{2,1,0:T(8,128)(2,1)} %maximum_select_fusion.pair_ref, ...), custom_call_target="tpu_custom_call" | custom-call | tf_op jit(solution)/shard_map/attention_backward/pallas_call | solution.py:162
  284.8 3.2 constant_dynamic-slice_fusion.12
  295.6 4.7 fusion.101
  300.4 2.2 add_convert_fusion
  304.3 9.0 %all-to-all-start.3 = ((bf16[16,320,256]{2,1,0:T(8,128)(2,1)}), bf16[16,320,256]{2,1,0:T(8,128)(2,1)}, u32[]{:S(2)}, u32[]{:S(2)}) async-start(bf16[16,320,256]{2,1,0:T(8,128)(2,1)} %pad_maximum_fusion.1), calls=%async_computation.3 | async-start | bytes 5242880 | tf_op jit(solution)/shard_map/all_to_all | solution.py:318
  313.4 4.7 fusion.102
  319.2 159.7 %all-reduce.4.cloned.1.call-done = (bf16[1088,128]{1,0:T(8,128)(2,1)}, bf16[128,1088]{0,1:T(8,128)(2,1)}, bf16[1088,128]{1,0:T(8,128)(2,1)}, bf16[128,4352]{1,0:...) async-done(((bf16[1088,128]{1,0:T(8,128)(2,1)}, bf16[128,1088]{0,1:T(8,128)(2,1)}, bf16[1088,128]{1,0:T(8,128)(2,1)}, bf16[128,4352]{1,0:T(8,128)(2,1)}, ...) | async-done | bytes 3342352 | tf_op jit(solution)/shard_map/psum | solution.py:452
  552.0 2.2 collective-permute-done.34
  (446 shorter events, 139.9 us)
Async XLA Ops:
  10.1 5.4 collective-permute-start
  10.6 15.5 %collective-permute-start.1 = (bf16[544,1088]{1,0:T(8,128)(2,1)}, bf16[544,1088]{1,0:T(8,128)(2,1)}, u32[]{:S(2)}, u32[]{:S(2)}) collective-permute-start(bf16[544,1088]{1,0:T(8,128)(2,1)} %param.33), channel_id=1, source_target_pairs={{0,1},{1,0},{2,3},{3,2},{4,5},{5,4},{6,7},{7,6},{8,9},{9,8},{10,11... | collective-permute-start | bytes 3551240 | tf_op jit(solution)/shard_map/ppermute | solution.py:297
  10.7 10.3 %collective-permute-start.3 = (bf16[544,1088]{1,0:T(8,128)(2,1)}, bf16[544,1088]{1,0:T(8,128)(2,1)}, u32[]{:S(2)}, u32[]{:S(2)}) collective-permute-start(bf16[544,1088]{1,0:T(8,128)(2,1)} %param.35), channel_id=1, source_target_pairs={{0,1},{1,0},{2,3},{3,2},{4,5},{5,4},{6,7},{7,6},{8,9},{9,8},{10,11... | collective-permute-start | bytes 3551240 | tf_op jit(solution)/shard_map/ppermute | solution.py:297
  11.2 12.3 %collective-permute-start.2 = (bf16[544,1088]{1,0:T(8,128)(2,1)}, bf16[544,1088]{1,0:T(8,128)(2,1)}, u32[]{:S(2)}, u32[]{:S(2)}) collective-permute-start(bf16[544,1088]{1,0:T(8,128)(2,1)} %param.34), channel_id=1, source_target_pairs={{0,1},{1,0},{2,3},{3,2},{4,5},{5,4},{6,7},{7,6},{8,9},{9,8},{10,11... | collective-permute-start | bytes 3551240 | tf_op jit(solution)/shard_map/ppermute | solution.py:297
  31.6 60.4 %all-to-all-start = ((bf16[16,320,256]{2,1,0:T(8,128)(2,1)}), bf16[16,320,256]{2,1,0:T(8,128)(2,1)}, u32[]{:S(2)}, u32[]{:S(2)}) async-start(bf16[16,320,256]{2,1,0:T(8,128)(2,1)} %pad_maximum_fusion), calls=%async_computation | async-start | bytes 5242880 | tf_op jit(solution)/shard_map/all_to_all | solution.py:318
  39.9 133.0 %collective-permute-start.7 = (bf16[4352,544]{0,1:T(8,128)(2,1)}, bf16[4352,544]{0,1:T(8,128)(2,1)}, u32[]{:S(2)}, u32[]{:S(2)}) collective-permute-start(bf16[4352,544]{0,1:T(8,128)(2,1)} %param.38), channel_id=1, source_target_pairs={{0,1},{1,0},{2,3},{3,2},{4,5},{5,4},{6,7},{7,6},{8,9},{9,8},{10,11... | collective-permute-start | bytes 14204936 | tf_op jit(solution)/shard_map/ppermute | solution.py:297
  95.1 4.9 collective-permute-start.4
  95.1 89.4 %collective-permute-start.5 = (bf16[544,1088]{1,0:T(8,128)(2,1)}, bf16[544,1088]{1,0:T(8,128)(2,1)}, u32[]{:S(2)}, u32[]{:S(2)}) collective-permute-start(bf16[544,1088]{1,0:T(8,128)(2,1)} %param.36), channel_id=1, source_target_pairs={{0,1},{1,0},{2,3},{3,2},{4,5},{5,4},{6,7},{7,6},{8,9},{9,8},{10,11... | collective-permute-start | bytes 3551240 | tf_op jit(solution)/shard_map/ppermute | solution.py:297
  95.6 95.1 %collective-permute-start.6 = (bf16[544,4352]{1,0:T(8,128)(2,1)}, bf16[544,4352]{1,0:T(8,128)(2,1)}, u32[]{:S(2)}, u32[]{:S(2)}) collective-permute-start(bf16[544,4352]{1,0:T(8,128)(2,1)} %param.37), channel_id=1, source_target_pairs={{0,1},{1,0},{2,3},{3,2},{4,5},{5,4},{6,7},{7,6},{8,9},{9,8},{10,11... | collective-permute-start | bytes 14204936 | tf_op jit(solution)/shard_map/ppermute | solution.py:297
  151.5 28.0 %all-to-all-start.1 = ((bf16[16,64,256]{2,1,0:T(8,128)(2,1)}), bf16[16,64,256]{2,1,0:T(8,128)(2,1)}, u32[]{:S(2)}, u32[]{:S(2)}) async-start(bf16[16,64,256]{2,1,0:T(8,128)(2,1)} %slice.148), calls=%async_computation.1 | async-start | bytes 1048576 | tf_op jit(solution)/shard_map/all_to_all | solution.py:318
  216.1 17.9 %all-to-all-start.2 = ((bf16[16,64,256]{2,1,0:T(8,128)(2,1)}), bf16[16,64,256]{2,1,0:T(8,128)(2,1)}, u32[]{:S(2)}, u32[]{:S(2)}) async-start(bf16[16,64,256]{2,1,0:T(8,128)(2,1)} %bitcast.21), calls=%async_computation.2 | async-start | bytes 1048576 | tf_op jit(solution)/shard_map/all_to_all | solution.py:318
  223.1 255.8 %all-reduce.4.cloned.1.call-start = ((), (), s32[]{:S(2)}) async-start(), calls=%async_computation.4 | async-start | bytes 6684672 | tf_op jit(solution)/shard_map/psum | solution.py:452
  288.1 12.3 %collective-permute-start.8 = (bf16[16,256,256]{2,1,0:T(8,128)(2,1)}, bf16[16,256,256]{2,1,0:T(8,128)(2,1)}, u32[]{:S(2)}, u32[]{:S(2)}) collective-permute-start(bf16[16,256,256]{2,1,0:T(8,128)(2,1)} %constant_dynamic-slice_fusion.12), channel_id=1, source_target_pairs={{0,1},{1,0},{2,3},{3,2},{4,5},{5,4},{6,7},{7,6},{8,9},{9,8},{10,11... | collective-permute-start | bytes 6291464 | tf_op jit(solution)/shard_map/ppermute | solution.py:297
  304.3 183.3 %all-to-all-start.3 = ((bf16[16,320,256]{2,1,0:T(8,128)(2,1)}), bf16[16,320,256]{2,1,0:T(8,128)(2,1)}, u32[]{:S(2)}, u32[]{:S(2)}) async-start(bf16[16,320,256]{2,1,0:T(8,128)(2,1)} %pad_maximum_fusion.1), calls=%async_computation.3 | async-start | bytes 5242880 | tf_op jit(solution)/shard_map/all_to_all | solution.py:318
  509.4 6.0 %collective-permute-start.10 = (bf16[576,128]{1,0:T(8,128)(2,1)S(1)}, bf16[576,128]{1,0:T(8,128)(2,1)S(1)}, u32[]{:S(2)}, u32[]{:S(2)}) collective-permute-start(bf16[576,128]{1,0:T(8,128)(2,1)S(1)} %constant_dynamic-slice_fusion.11), channel_id=1, source_target_pairs={{0,2},{2,0},{4,6},{6,4},{8,10},{10,8},{12,14},{14,12},{16,18},{18,... | collective-permute-start | bytes 442376 | tf_op jit(solution)/shard_map/ppermute | solution.py:196
  511.0 6.0 %collective-permute-start.18 = (bf16[576,128]{1,0:T(8,128)(2,1)S(1)}, bf16[576,128]{1,0:T(8,128)(2,1)S(1)}, u32[]{:S(2)}, u32[]{:S(2)}) collective-permute-start(bf16[576,128]{1,0:T(8,128)(2,1)S(1)} %constant_dynamic-slice_fusion.7), channel_id=1, source_target_pairs={{0,4},{2,6},{4,0},{6,2},{8,12},{10,14},{12,8},{14,10},{16,20},{18,... | collective-permute-start | bytes 442376 | tf_op jit(solution)/shard_map/ppermute | solution.py:196
  512.1 6.4 %collective-permute-start.26 = (bf16[576,128]{1,0:T(8,128)(2,1)S(1)}, bf16[576,128]{1,0:T(8,128)(2,1)S(1)}, u32[]{:S(2)}, u32[]{:S(2)}) collective-permute-start(bf16[576,128]{1,0:T(8,128)(2,1)S(1)} %constant_dynamic-slice_fusion.3), channel_id=1, source_target_pairs={{0,8},{2,10},{4,12},{6,14},{8,0},{10,2},{12,4},{14,6},{16,24},{18,... | collective-permute-start | bytes 442376 | tf_op jit(solution)/shard_map/ppermute | solution.py:196
  526.2 4.8 collective-permute-start.21
  527.8 4.9 collective-permute-start.29
  532.7 4.8 collective-permute-start.30
  538.6 5.0 collective-permute-start.16
  543.7 5.2 collective-permute-start.17
  544.7 5.2 collective-permute-start.25
  546.4 5.2 collective-permute-start.33
  (112 other events, 824.7 us)
Sparse Core Ops, SparseCore 0:
  295.7 183.1 all-reduce.3

commit v2 on v1

v2 whole, which is shorter than its diff:
```python
import functools
import math

import jax
import jax.numpy as jnp
from jax import lax
from jax.experimental import pallas as pl
from jax.experimental.pallas import tpu as pltpu
from jax.sharding import PartitionSpec as P

HEAD = 64
RANK = 16
DOC_MAX = 4096


EPSILON = 1e-05
NEG_FILL = -1e30
SCALING = HEAD ** (-0.5)
SWAP = [(0, 1), (1, 0)]
VMEM_BYTES = 48 * 1024 * 1024


def norm_parts(values, gain, shift):
    row_mean = jnp.mean(values, axis=-1, keepdims=True)
    centered = values - row_mean
    variance = jnp.mean(centered * centered, axis=-1, keepdims=True)
    inverse = lax.rsqrt(variance + EPSILON)
    normed = centered * inverse
    return (normed * gain + shift, normed, inverse)


def norm_back(grad, normed, inverse, gain):
    scaled = grad * gain
    return inverse * (
        scaled
        - jnp.mean(scaled, axis=-1, keepdims=True)
        - normed * jnp.mean(scaled * normed, axis=-1, keepdims=True)
    )


def dot(left, right, lc=1, rc=0):
    return lax.dot_general(
        left, right, (((lc,), (rc,)), ((), ())), preferred_element_type=jnp.float32
    )


def group_lanes(meta_ref, starts_ref, g, rows, skip):
    lanes = lax.broadcasted_iota(jnp.int32, (1, starts_ref.shape[2]), 1)
    return starts_ref[g], meta_ref[g, 2] + lanes + jnp.where(lanes >= rows, skip, 0)


def side_by_side(ref, first, count):
    return jnp.concatenate([ref[first + k, 0:HEAD, :] for k in range(count)], axis=1)


def masked(scores, j, first_key, doc_start, query_pos):
    size = scores.shape[0]
    key_pos = first_key + j * size + lax.broadcasted_iota(jnp.int32, (size, 1), 0)
    allowed = (key_pos >= doc_start) & (key_pos <= query_pos)
    return jnp.where(allowed, scores, NEG_FILL)


def forward_kernel(
    pair_at, first_chunk, per_group, meta_ref, starts_ref, query_ref, own_ref, other_ref,
    low_ref, mixed_ref, lse_ref, rows_ref, values_ref,
):
    groups, _, lanes = starts_ref.shape
    rows = own_ref.shape[2]
    size = 2 * rows
    core, first_key = meta_ref[0, 3], meta_ref[0, 4]

    def spread(j, carry):
        for ref, side in ((own_ref, core), (other_ref, 1 - core)):
            spot = pl.multiple_of(side * rows, rows)
            pair = ref[j, pair_at : pair_at + 2 * HEAD, :]
            rows_ref[pl.ds(pl.multiple_of(j * size + spot, rows), rows), :] = pair.T
            values_ref[j, :, pl.ds(spot, rows)] = pair[HEAD:]
        return carry

    lax.fori_loop(meta_ref[0, 5], meta_ref[0, 6] + 1, spread, 0)

    def group(g, carry):
        query = side_by_side(query_ref, first_chunk + g * per_group, per_group)
        query = (query.astype(jnp.float32) * SCALING).astype(jnp.bfloat16)
        query = jnp.concatenate([query, jnp.zeros_like(query)], axis=0)
        doc_start, query_pos = group_lanes(meta_ref, starts_ref, g, rows, size - rows)

        def block(j, state):
            row_max, row_sum, total = state
            keys = rows_ref[pl.ds(pl.multiple_of(j * size, size), size), :]
            scores = masked(dot(keys, query), j, first_key, doc_start, query_pos)
            new_max = jnp.maximum(row_max, jnp.max(scores, axis=0, keepdims=True))
            probs = jnp.exp(scores - new_max)
            shrink = jnp.exp(row_max - new_max)
            row_sum = row_sum * shrink + jnp.sum(probs, axis=0, keepdims=True)
            total = total * shrink + dot(values_ref[j], probs.astype(jnp.bfloat16))
            return new_max, row_sum, total

        state = (
            jnp.full((1, lanes), NEG_FILL, jnp.float32),
            jnp.zeros((1, lanes), jnp.float32),
            jnp.zeros((HEAD, lanes), jnp.float32),
        )
        row_max, row_sum, total = lax.fori_loop(meta_ref[g, 0], meta_ref[g, 1] + 1, block, state)
        mixed = total / row_sum
        mixed_ref[g] = mixed
        for k in range(per_group):
            low_ref[g * per_group + k] = mixed[:, k * rows : (k + 1) * rows].astype(jnp.bfloat16)
        lse_ref[g] = row_max + jnp.log(row_sum)
        return carry

    lax.fori_loop(0, groups, group, 0)


def backward_kernel(
    pair_at, first_chunk, per_group, meta_ref, starts_ref, query_ref, own_ref, other_ref,
    rows_ref, grad_ref, mixed_ref, lse_ref, dq_ref, kept_ref, sent_ref, keys_ref, sum_ref,
):
    groups, _, lanes = starts_ref.shape
    rows = own_ref.shape[2]
    size = 2 * rows
    core, first_key = meta_ref[0, 3], meta_ref[0, 4]

    def prepare(j, carry):
        for ref, side in ((own_ref, core), (other_ref, 1 - core)):
            spot = pl.multiple_of(side * rows, rows)
            keys_ref[j, :, pl.ds(spot, rows)] = ref[j, pair_at : pair_at + HEAD, :]
        return carry

    lax.fori_loop(meta_ref[0, 5], meta_ref[0, 6] + 1, prepare, 0)
    sum_ref[...] = jnp.zeros(sum_ref.shape, jnp.float32)

    def group(g, carry):
        query = side_by_side(query_ref, first_chunk + g * per_group, per_group)
        query = (query.astype(jnp.float32) * SCALING).astype(jnp.bfloat16)
        grad = side_by_side(grad_ref, g * per_group, per_group)
        nothing = jnp.zeros_like(query)
        query_low = jnp.concatenate([query, nothing], axis=0)
        grad_high = jnp.concatenate([nothing, grad], axis=0)
        both = jnp.concatenate([query_low, grad_high], axis=1).T
        delta = jnp.sum(grad.astype(jnp.float32) * mixed_ref[g], axis=0, keepdims=True)
        lse = lse_ref[g]
        doc_start, query_pos = group_lanes(meta_ref, starts_ref, g, rows, size - rows)

        def block(j, total):
            spot = pl.ds(pl.multiple_of(j * size, size), size)
            pair = rows_ref[spot, :]
            scores = masked(dot(pair, query_low), j, first_key, doc_start, query_pos)
            probs = jnp.exp(scores - lse)
            prob_grad = dot(pair, grad_high)
            score_grad = (probs * (prob_grad - delta)).astype(jnp.bfloat16)
            sum_ref[spot, :] += dot(
                jnp.concatenate([score_grad, probs.astype(jnp.bfloat16)], axis=1), both
            )
            return total + dot(keys_ref[j], score_grad)

        total = lax.fori_loop(
            meta_ref[g, 0], meta_ref[g, 1] + 1, block, jnp.zeros((HEAD, lanes), jnp.float32)
        )
        total = (total * SCALING).astype(jnp.bfloat16)
        for k in range(per_group):
            dq_ref[g * per_group + k] = total[:, k * rows : (k + 1) * rows]
        return carry

    lax.fori_loop(0, groups, group, 0)

    def finish(j, carry):
        for ref, side in ((kept_ref, core), (sent_ref, 1 - core)):
            spot = pl.ds(pl.multiple_of(j * size + side * rows, rows), rows)
            ref[j] = sum_ref[spot, :].T.astype(ref.dtype)
        return carry

    lax.fori_loop(0, kept_ref.shape[0], finish, 0)


def cost(microseconds):
    return pl.CostEstimate(
        flops=microseconds * 1_000_000_000, bytes_accessed=microseconds * 1_000_000, transcendentals=0
    )


SMEM_SPEC = pl.BlockSpec(memory_space=pltpu.SMEM)
VMEM_SPEC = pl.BlockSpec(memory_space=pltpu.VMEM)


def attention_forward(plan, query, own, other, name, microseconds):
    meta, starts, pair_at, first_chunk, per_group = plan
    groups, _, lanes = starts.shape
    blocks, _, rows = own.shape
    return pl.pallas_call(
        functools.partial(forward_kernel, pair_at, first_chunk, per_group),
        out_shape=(
            jax.ShapeDtypeStruct((groups * per_group, HEAD, rows), jnp.bfloat16),
            jax.ShapeDtypeStruct((groups, HEAD, lanes), jnp.float32),
            jax.ShapeDtypeStruct((groups, 1, lanes), jnp.float32),
            jax.ShapeDtypeStruct((blocks * 2 * rows, 2 * HEAD), jnp.bfloat16),
        ),
        in_specs=[SMEM_SPEC] + [VMEM_SPEC] * 4,
        out_specs=(VMEM_SPEC,) * 4,
        scratch_shapes=[pltpu.VMEM((blocks, HEAD, 2 * rows), jnp.bfloat16)],
        compiler_params=pltpu.CompilerParams(vmem_limit_bytes=VMEM_BYTES),
        cost_estimate=cost(microseconds),
        name=name,
    )(meta, starts, query, own, other)


def attention_backward(plan, query, own, other, pair_rows, grad, mixed, lse, name, microseconds):
    meta, starts, pair_at, first_chunk, per_group = plan
    groups, _, lanes = starts.shape
    blocks, _, rows = own.shape
    return pl.pallas_call(
        functools.partial(backward_kernel, pair_at, first_chunk, per_group),
        out_shape=(
            jax.ShapeDtypeStruct((groups * per_group, HEAD, rows), jnp.bfloat16),
            jax.ShapeDtypeStruct((blocks, 2 * HEAD, rows), jnp.float32),
            jax.ShapeDtypeStruct((blocks, 2 * HEAD, rows), jnp.bfloat16),
        ),
        in_specs=[SMEM_SPEC] + [VMEM_SPEC] * 8,
        out_specs=(VMEM_SPEC,) * 3,
        scratch_shapes=[
            pltpu.VMEM((blocks, HEAD, 2 * rows), jnp.bfloat16),
            pltpu.VMEM((blocks * 2 * rows, 2 * HEAD), jnp.float32),
        ],
        compiler_params=pltpu.CompilerParams(vmem_limit_bytes=VMEM_BYTES),
        cost_estimate=cost(microseconds),
        name=name,
    )(meta, starts, query, own, other, pair_rows, grad, mixed, lse)


def gelu_parts(value):
    scale = (2.0 / math.pi) ** 0.5
    square = value * value
    bent = jnp.tanh(scale * value * (1.0 + 0.044715 * square))
    upper = 0.5 * (1.0 + bent)
    slope = 0.5 * value * (1.0 - bent * bent) * scale * (1.0 + 3 * 0.044715 * square)
    return value * upper, upper + slope


def column_norm(values, gain, shift):
    row_mean = jnp.mean(values, axis=0, keepdims=True)
    centered = values - row_mean
    variance = jnp.mean(centered * centered, axis=0, keepdims=True)
    inverse = lax.rsqrt(variance + EPSILON)
    normed = centered * inverse
    return (normed * gain + shift, normed, inverse)


def column_norm_back(grad, normed, inverse, gain):
    scaled = grad * gain
    return inverse * (
        scaled
        - jnp.mean(scaled, axis=0, keepdims=True)
        - normed * jnp.mean(scaled * normed, axis=0, keepdims=True)
    )


def middle_kernel(
    core_ref, mixed_ref, stream_ref, cotangent_ref, mask_ref, gains_ref,
    out_own_ref, out_other_ref, a_out_ref, b_out_ref, a_up_ref, b_down_ref,
    up_own_ref, up_other_ref, b_up_ref, down_own_ref, down_other_ref, a_down_ref,
    output_ref, middle_grad_ref, mixed_grad_ref,
    packed_ref,
    middle_ref, hidden_ref, hidden_own_ref, hidden_other_ref, cot_own_ref, cot_other_ref,
    inner_out_ref, inner_up_ref, down_grad_ref, inner_down_ref, up_grad_ref,
    down_ref, back_ref,
):
    tile, width, wide = up_own_ref.shape[1], mixed_ref.shape[0], packed_ref.shape[0]
    wide = (wide - 4 * width) // 2
    step = pl.program_id(0)
    core = core_ref[0]
    half = out_own_ref.shape[0]
    low = jnp.bfloat16
    own_rows = pl.ds(pl.multiple_of(core * half, 32), half)
    other_rows = pl.ds(pl.multiple_of((1 - core) * half, 32), half)

    @pl.when(step == 0)
    def _():
        mask = mask_ref[...]
        mixed_own = mixed_ref[own_rows, :].T
        mixed_other = mixed_ref[other_rows, :].T
        inner_out = (mask * (dot(mixed_ref[...].T, a_out_ref[...]))).astype(low)
        inner_out_ref[...] = inner_out
        branch = dot(mixed_own, out_own_ref[...]) + dot(mixed_other, out_other_ref[...])
        branch = branch.T + dot(b_out_ref[...], inner_out.T)
        middle = stream_ref[...].astype(jnp.float32) + branch
        middle_ref[...] = middle
        hidden = column_norm(middle, gains_ref[:, 2:3], gains_ref[:, 3:4])[0].astype(low)
        hidden_ref[...] = hidden
        hidden_own_ref[...] = hidden_ref[own_rows, :].T
        hidden_other_ref[...] = hidden_ref[other_rows, :].T
        inner_up_ref[...] = (mask * dot(hidden.T, a_up_ref[...])).astype(low)
        cot_own_ref[...] = cotangent_ref[own_rows, :].T
        cot_other_ref[...] = cotangent_ref[other_rows, :].T
        inner_grad = dot(cotangent_ref[...].T, b_down_ref[...])
        down_grad_ref[...] = inner_grad.astype(low) * mask.astype(low)
        for ref in (inner_down_ref, up_grad_ref, down_ref, back_ref):
            ref[...] = jnp.zeros(ref.shape, ref.dtype)

    up_own, up_other, down_own, down_other = (
        ref[...] for ref in (up_own_ref, up_other_ref, down_own_ref, down_other_ref)
    )
    inner_up, down_grad, a_down = inner_up_ref[...], down_grad_ref[...], a_down_ref[...]
    upward = (
        dot(hidden_own_ref[...], up_own)
        + dot(hidden_other_ref[...], up_other)
        + dot(inner_up, b_up_ref[...])
    )
    active_grad = (
        dot(cot_own_ref[...], down_own)
        + dot(cot_other_ref[...], down_other)
        + dot(down_grad, a_down.T)
    )
    active, slope = gelu_parts(upward)
    active = active.astype(low)
    up_grad = (active_grad * slope).astype(low)
    active_t, up_grad_t = active.T, up_grad.T
    down_ref[own_rows, :] += dot(down_own, active_t)
    down_ref[other_rows, :] += dot(down_other, active_t)
    back_ref[own_rows, :] += dot(up_own, up_grad_t)
    back_ref[other_rows, :] += dot(up_other, up_grad_t)
    inner_down_ref[...] += dot(active, a_down)
    up_grad_ref[...] += dot(b_up_ref[...], up_grad_t)
    here = pl.multiple_of(step * tile, tile)
    packed_ref[pl.ds(here, tile), :] = dot(up_grad_t, inner_up).astype(low)
    packed_ref[pl.ds(wide + here, tile), :] = dot(active_t, down_grad).astype(low)

    @pl.when(step == pl.num_programs(0) - 1)
    def _():
        mask = mask_ref[...]
        mask_low = mask.astype(low)
        cotangent = cotangent_ref[...]
        inner_down = (mask * inner_down_ref[...]).astype(low)
        middle = middle_ref[...]
        down = down_ref[...] + dot(b_down_ref[...], inner_down.T)
        output_ref[...] = (middle + down).astype(low)
        narrow = [packed_ref.at[pl.ds(2 * wide + k * width, width), :] for k in range(4)]
        narrow[0][...] = dot(cotangent, inner_down).astype(low)
        inner_grad = up_grad_ref[...].astype(low).T * mask_low
        hidden_grad = back_ref[...] + dot(a_up_ref[...], inner_grad.T)
        narrow[1][...] = dot(hidden_ref[...], inner_grad).astype(low)
        gain = gains_ref[:, 2:3]
        _, normed, inverse = column_norm(middle, gain, gain)
        middle_grad = cotangent.astype(jnp.float32) + column_norm_back(
            hidden_grad, normed, inverse, gain
        )
        middle_grad_ref[...] = middle_grad
        branch = middle_grad.astype(low)
        out_grad = dot(branch.T, b_out_ref[...]).astype(low) * mask_low
        turned = out_grad.T
        for rows, weight in ((own_rows, out_own_ref[...]), (other_rows, out_other_ref[...])):
            back = dot(weight, branch) + dot(a_out_ref[rows, :], turned)
            mixed_grad_ref[rows, :] = back.astype(low)
        narrow[2][...] = dot(mixed_ref[...], out_grad).astype(low)
        narrow[3][...] = dot(branch, inner_out_ref[...]).astype(low)


def middle_part(
    core, mixed_t, tokens_t, cotangent_t, mask, gains_t, out_pair, a_out, b_out_t, a_up, b_down_t,
    up_pair, b_up, down_pair_t, a_down,
):
    width, rows = mixed_t.shape
    half = width // 2
    inner, wide = b_up.shape
    tile = 2 * inner
    low = jnp.bfloat16

    def fixed(shape):
        return pl.BlockSpec(shape, lambda f: (0,) * len(shape), pipeline_mode=pl.Buffered(1))

    def out(shape):
        return pl.BlockSpec(shape, lambda f: (0,) * len(shape))

    def columns(height):
        return pl.BlockSpec((height, tile), lambda f: (0, f))

    def lines(length):
        return pl.BlockSpec((tile, length), lambda f: (f, 0))

    operands = (
        mixed_t, tokens_t, cotangent_t, mask, gains_t, *out_pair, a_out, b_out_t, a_up, b_down_t
    )
    shapes = (
        ((width, rows), low), ((width, rows), jnp.float32), ((width, rows), low),
        ((2 * wide + 4 * width, inner), low),
    )
    return pl.pallas_call(
        middle_kernel,
        grid=(wide // tile,),
        out_shape=tuple(jax.ShapeDtypeStruct(*item) for item in shapes),
        in_specs=[SMEM_SPEC]
        + [fixed(item.shape) for item in operands]
        + [columns(half), columns(half), columns(inner), columns(half), columns(half), lines(inner)],
        out_specs=tuple(out(item[0]) for item in shapes),
        scratch_shapes=[
            pltpu.VMEM((width, rows), jnp.float32),
            pltpu.VMEM((width, rows), low),
            *[pltpu.VMEM((rows, half), low)] * 4,
            *[pltpu.VMEM((rows, inner), low)] * 3,
            pltpu.VMEM((rows, inner), jnp.float32),
            pltpu.VMEM((inner, rows), jnp.float32),
            *[pltpu.VMEM((width, rows), jnp.float32)] * 2,
        ],
        compiler_params=pltpu.CompilerParams(
            vmem_limit_bytes=VMEM_BYTES, dimension_semantics=("arbitrary",)
        ),
        cost_estimate=cost(1),
        name="middle_part",
    )(core, *operands, *up_pair, b_up, *down_pair_t, a_down)


def summed_rows(packed, cycle_size):
    wide = packed.shape[0]
    bits = cycle_size.bit_length() - 1
    unit = 3 * 2 * cycle_size * 8
    rows = -(-wide // unit) * unit
    packed = jnp.pad(packed, ((0, rows - wide), (0, 0)))
    place, core = lax.axis_index("ctx"), lax.axis_index("wsh")

    def halves(array, bit):
        size = array.shape[0] // 2
        kept = lax.dynamic_slice_in_dim(array, bit * size, size, 0)
        sent = lax.dynamic_slice_in_dim(array, (1 - bit) * size, size, 0)
        return kept, sent

    def joined(own, other, bit):
        size = own.shape[0]
        whole = jnp.concatenate([own, own], axis=0)
        return lax.dynamic_update_slice_in_dim(whole, other, (1 - bit) * size, 0)

    def exchange(array, bit):
        return lax.ppermute(array, "ctx", [(i, i ^ (1 << bit)) for i in range(cycle_size)])

    kept, sent = halves(packed, core)
    mine = kept + lax.ppermute(sent, "wsh", SWAP)
    third = mine.shape[0] // 3
    parts = [mine[i * third : (i + 1) * third] for i in range(3)]
    low = min(3, bits)
    orders = [[(s + i) % low for s in range(low)] + list(range(low, bits)) for i in range(3)]
    for step in range(bits):
        following = []
        for part, order in zip(parts, orders):
            kept, sent = halves(part, (place >> order[step]) & 1)
            following.append(kept + exchange(sent, order[step]))
        parts = following
    for step in reversed(range(bits)):
        parts = [
            joined(part, exchange(part, order[step]), (place >> order[step]) & 1)
            for part, order in zip(parts, orders)
        ]
    mine = jnp.concatenate(parts, axis=0)
    return joined(mine, lax.ppermute(mine, "wsh", SWAP), core)[:wide]


def halved(array, bit, cycle_size):
    size = array.shape[0] // 2
    side = (lax.axis_index("ctx") >> bit) & 1
    kept = lax.dynamic_slice_in_dim(array, side * size, size, 0)
    sent = lax.dynamic_slice_in_dim(array, (1 - side) * size, size, 0)
    return kept + lax.ppermute(sent, "ctx", [(i, i ^ (1 << bit)) for i in range(cycle_size)])


def local(
    tokens_in,
    doc_lengths,
    doc_adapter,
    norm1_gain,
    norm1_bias,
    norm2_gain,
    norm2_bias,
    w_query,
    w_key,
    w_value,
    w_out,
    w_up,
    w_down,
    a_query,
    b_query,
    a_key,
    b_key,
    a_value,
    b_value,
    a_out,
    b_out,
    a_up,
    b_up,
    a_down,
    b_down,
    cotangent,
):
    group_size = lax.axis_size("wsh")
    cycle_size = lax.axis_size("ctx")
    tok_dev, width_all = tokens_in.shape
    head_count = width_all // HEAD
    block_len = tok_dev * group_size
    hop_count = (DOC_MAX + block_len - 2) // block_len
    span = head_count - 1
    cycle_pos = lax.axis_index("ctx")
    core = lax.axis_index("wsh")
    half = width_all // group_size

    first_row = cycle_pos * block_len + core * tok_dev
    doc_ends = jnp.cumsum(doc_lengths)
    doc_starts = doc_ends - doc_lengths
    query_pos = first_row + jnp.arange(tok_dev, dtype=jnp.int32)
    query_docs = jnp.sum((doc_ends[None, :] <= query_pos[:, None]).astype(jnp.int32), axis=1)
    doc_numbers = jnp.arange(doc_lengths.shape[0], dtype=jnp.int32)
    token_adapter = jnp.sum(
        jnp.where(query_docs[:, None] == doc_numbers[None, :], doc_adapter[None, :], 0), axis=1
    )
    columns = jnp.arange(a_query.shape[1], dtype=jnp.int32) // RANK
    adapter_mask = (token_adapter[:, None] == columns[None, :]).astype(jnp.float32)
    mask_low = adapter_mask.astype(jnp.bfloat16)

    team = cycle_pos // span
    past = hop_count if cycle_size > span else 0
    first_key = (team * span - past) * block_len
    key_blocks = past + span

    def plan(chunk_pos, pair_at, first_chunk, per_group):
        groups = chunk_pos.shape[0] // per_group
        row_pos = chunk_pos[:, None] + jnp.arange(tok_dev, dtype=jnp.int32)[None, :]
        began = doc_starts[None, None, :] <= row_pos[:, :, None]
        row_starts = jnp.max(jnp.where(began, doc_starts[None, None, :], 0), axis=2)
        row_starts = row_starts.reshape(groups, 1, per_group * tok_dev)
        chunk_pos = chunk_pos.reshape(groups, per_group)
        first = (row_starts[:, 0, 0] - first_key) // block_len
        last = (chunk_pos[:, -1] - first_key) // block_len
        same = jnp.ones((groups,), jnp.int32)
        whole = per_group > 1
        meta = [
            first,
            last,
            chunk_pos[:, 0],
            same * core,
            same * first_key,
            same * 0 if whole else first,
            same * (key_blocks - 1) if whole else last,
        ]
        meta = jnp.stack(meta, axis=1).astype(jnp.int32)
        return meta, row_starts.astype(jnp.int32), pair_at, first_chunk, per_group

    team_pos = (team * span + jnp.arange(span, dtype=jnp.int32)) * block_len + core * tok_dev
    main_plan = plan(team_pos.astype(jnp.int32), HEAD, past, 2)
    last_plan = plan(first_row[None].astype(jnp.int32), 0, 0, 1)

    def swap(array):
        return lax.ppermute(array, "wsh", SWAP)

    def ordered(own, other, axis):
        return jnp.where(
            core == 0,
            jnp.concatenate([own, other], axis=axis),
            jnp.concatenate([other, own], axis=axis),
        )

    def own_other(array):
        return (
            lax.dynamic_slice_in_dim(array, core * half, half, 1),
            lax.dynamic_slice_in_dim(array, (1 - core) * half, half, 1),
        )

    if cycle_size > span:
        teams = [[t * span + i for i in range(span)] for t in range(cycle_size // span)]
    else:
        teams = None

    def exchange(blocks):
        return lax.all_to_all(blocks, "ctx", 0, 0, tiled=True, axis_index_groups=teams)

    gains = jnp.stack([norm1_gain, norm1_bias, norm2_gain, norm2_bias])
    gains = ordered(gains, swap(gains), 1).astype(jnp.float32)
    weights = [w_query, w_key, w_value, w_out, w_up, w_down.T]
    others = [swap(item) for item in weights]

    stream = tokens_in.astype(jnp.float32)
    norm_one, normed_one, inverse_one = norm_parts(stream, gains[0], gains[1])
    hidden_one = norm_one.astype(jnp.bfloat16)
    hidden_own, hidden_other = own_other(hidden_one)

    def projected(number, down_a, up_b):
        inner = (adapter_mask * dot(hidden_one, down_a)).astype(jnp.bfloat16)
        total = (
            dot(weights[number], hidden_own, 0, 1)
            + dot(others[number], hidden_other, 0, 1)
            + dot(up_b, inner, 0, 1)
        )
        return total.astype(jnp.bfloat16).reshape(head_count, HEAD, tok_dev), inner

    query_t, inner_query = projected(0, a_query, b_query)
    keys_t, inner_key = projected(1, a_key, b_key)
    values_t, inner_value = projected(2, a_value, b_value)

    ahead = [(i, i + span) for i in range(cycle_size - span)]
    back = [(i + span, i) for i in range(cycle_size - span)]

    def with_past(blocks):
        if not past:
            return blocks
        return jnp.concatenate([lax.ppermute(blocks[span - past :], "ctx", ahead), blocks], axis=0)

    incoming = exchange(jnp.concatenate([query_t[:span], keys_t[:span], values_t[:span]], axis=1))
    last_pair = jnp.concatenate([keys_t[span:], values_t[span:]], axis=1)
    incoming, last_pair = lax.optimization_barrier((incoming, last_pair))
    own = with_past(incoming)
    other = swap(own)
    last_own = exchange(jnp.broadcast_to(last_pair, (span, 2 * HEAD, tok_dev)))
    low_main, mixed_main, lse_main, rows_main = attention_forward(
        main_plan, own, own, other, "attention_forward", 30
    )
    low_main, last_own = lax.optimization_barrier((low_main, last_own))
    last_own = with_past(last_own)
    last_other = swap(last_own)
    low_last, mixed_last, lse_last, rows_last = attention_forward(
        last_plan, query_t[span:], last_own, last_other, "last_forward", 3
    )
    mixed_t = jnp.concatenate([exchange(low_main), low_last], axis=0)
    mixed_t = mixed_t.reshape(width_all, tok_dev)

    output_t, middle_grad_t, mixed_grad_t, early = middle_part(
        core[None], mixed_t, tokens_in.T, cotangent.T, adapter_mask, gains.T, (w_out, others[3]),
        a_out, b_out.T, a_up, b_down.T, (w_up, others[4]), b_up, (w_down.T, others[5]), a_down,
    )
    mixed_grad_t = mixed_grad_t.reshape(head_count, HEAD, tok_dev)

    bits = cycle_size.bit_length() - 1
    lanes = early.shape[1]
    share = early.shape[0] // 2
    early_sent = lax.dynamic_slice_in_dim(early, (1 - core) * share, share, 0)
    early_kept = lax.dynamic_slice_in_dim(early, core * share, share, 0)
    early = halved(early_kept + swap(early_sent), 0, cycle_size)

    def pair_back(kept, sent):
        total = kept + swap(sent).astype(jnp.float32)
        if past:
            returned = lax.ppermute(total[:past].astype(jnp.bfloat16), "ctx", back)
            total = total[past:].at[span - past :].add(returned.astype(jnp.float32))
        return total.astype(jnp.bfloat16)

    dq_last, kept_last, sent_last = attention_backward(
        last_plan, query_t[span:], last_own, last_other, rows_last,
        mixed_grad_t[span:], mixed_last, lse_last, "last_backward", 6,
    )
    grad_main = exchange(mixed_grad_t[:span])
    dpair_last = pair_back(kept_last, sent_last)
    grad_main, dpair_last, early = lax.optimization_barrier((grad_main, dpair_last, early))
    dpair_last = exchange(dpair_last)
    dq_main, kept_main, sent_main = attention_backward(
        main_plan, own, own, other, rows_main, grad_main, mixed_main, lse_main,
        "attention_backward", 40
    )
    dq_main, dpair_last, early = lax.optimization_barrier((dq_main, dpair_last, early))
    for bit in range(1, bits):
        early = halved(early, bit, cycle_size)
    early = lax.all_gather(early, ("ctx", "wsh"), axis=0, tiled=False)
    last_sum = jnp.sum(dpair_last.astype(jnp.float32), axis=0).astype(jnp.bfloat16)
    incoming_back = exchange(jnp.concatenate([dq_main, pair_back(kept_main, sent_main)], axis=1))

    def gathered(first, last):
        main = incoming_back[:, first : first + HEAD].reshape(span * HEAD, tok_dev)
        return jnp.concatenate([main, last], axis=0)

    grads_t = [
        gathered(0, dq_last[0]),
        gathered(HEAD, last_sum[:HEAD]),
        gathered(2 * HEAD, last_sum[HEAD:]),
    ]

    own_sum, other_sum, adapter_sum = 0.0, 0.0, 0.0
    late = []
    for number, (grad_t, down_a, up_b, inner) in enumerate(
        zip(
            grads_t,
            (a_query, a_key, a_value),
            (b_query, b_key, b_value),
            (inner_query, inner_key, inner_value),
        )
    ):
        inner_grad = dot(grad_t, up_b, 0, 1).astype(jnp.bfloat16) * mask_low
        own_sum = own_sum + dot(grad_t, weights[number], 0, 1)
        other_sum = other_sum + dot(grad_t, others[number], 0, 1)
        adapter_sum = adapter_sum + dot(inner_grad, down_a, 1, 1)
        late.append(dot(hidden_one, inner_grad, 0, 0))
        late.append(dot(grad_t, inner, 1, 0))
    hidden_one_grad = ordered(own_sum, other_sum, 1) + adapter_sum
    stream_grad = middle_grad_t.T + norm_back(hidden_one_grad, normed_one, inverse_one, gains[0])
    grad_in = stream_grad.astype(jnp.bfloat16)

    norm_factor = (tok_dev * group_size * cycle_size) ** (-0.5)
    packed = jnp.concatenate([item.astype(jnp.bfloat16) for item in late], axis=0)
    late_sum, early = lax.optimization_barrier((summed_rows(packed, cycle_size), early))
    early = early.reshape((2,) * (bits + 1) + (share // cycle_size, lanes))
    early = jnp.transpose(early, tuple(reversed(range(bits + 1))) + (bits + 1, bits + 2))
    early = early.reshape(group_size * share, lanes)
    early = early.astype(jnp.float32) * norm_factor
    wide = b_up.shape[1]
    narrow = [early[2 * wide + k * width_all : 2 * wide + (k + 1) * width_all] for k in range(4)]
    late_sum = late_sum.astype(jnp.float32) * norm_factor
    late_sum = [late_sum[i * width_all : (i + 1) * width_all] for i in range(6)]
    return (
        output_t.T,
        grad_in,
        late_sum[0],
        late_sum[1].T,
        late_sum[2],
        late_sum[3].T,
        late_sum[4],
        late_sum[5].T,
        narrow[2],
        narrow[3].T,
        narrow[1],
        early[:wide].T,
        early[wide : 2 * wide],
        narrow[0].T,
    )


def solution(mesh):
    return jax.shard_map(
        local,
        mesh=mesh,
        in_specs=(
            P(("ctx", "wsh"), None),
            P(),
            P(),
            P("wsh"),
            P("wsh"),
            P("wsh"),
            P("wsh"),
            P("wsh", None),
            P("wsh", None),
            P("wsh", None),
            P("wsh", None),
            P("wsh", None),
            P(None, "wsh"),
            P(),
            P(),
            P(),
            P(),
            P(),
            P(),
            P(),
            P(),
            P(),
            P(),
            P(),
            P(),
            P(("ctx", "wsh"), None),
        ),
        out_specs=(
            P(("ctx", "wsh"), None),
            P(("ctx", "wsh"), None),
            P(),
            P(),
            P(),
            P(),
            P(),
            P(),
            P(),
            P(),
            P(),
            P(),
            P(),
            P(),
        ),
        check_vma=False,
    )
```

time: 574 us -> 422 us (0.74); the launches traced: 564 us -> 419 us
  waiting for transfers between devices: 231 us -> 91 us
  matrix products: 84.1 us -> 19.7 us
  starting transfers between devices: 75.3 us -> 103 us
  Pallas kernels: 89.9 us -> 117 us
  local copies, waits for them, and re-layouts: 34.8 us -> 45.6 us
    psum x1 -> x0, waiting for transfers between devices: 160 us -> none  [local(): lax.psum(tuple((item.astype(jnp.bfloat16) for item in (dot(mixed_low, out...]
    dot_general x60 -> x30, matrix products: 84.1 us -> 19.7 us  [dot(): lax.dot_general(left, right, (((lc,), (rc,)), ((), ())), preferred_elemen...]
    ppermute x0 -> x4, waiting for transfers between devices: none -> 34.7 us  [halved(): lax.ppermute(sent, 'ctx', [(i, i ^ 1 << bit) for i in range(cycle_size)])]
    pallas_call x2 -> x5, Pallas kernels: 89.9 us -> 117 us  [the longest x2 49 us: attention_backward(): pl.pallas_call(functools.partial(backward_kernel, pair_at, first_chunk, p...]
    all_to_all x4 -> x6, waiting for transfers between devices: 59.4 us -> 39.6 us  [exchange(): lax.all_to_all(blocks, 'ctx', 0, 0, tiled=True, axis_index_groups=teams)]
    unnamed x193 -> x164, local copies, waits for them, and re-layouts: 13 us -> 23.5 us
    all_gather x0 -> x1, starting transfers between devices: none -> 9.75 us  [local(): early = lax.all_gather(early, ('ctx', 'wsh'), axis=0, tiled=False)]
    ppermute x0 -> x4, starting transfers between devices: none -> 9.52 us  [halved(): lax.ppermute(sent, 'ctx', [(i, i ^ 1 << bit) for i in range(cycle_size)])]
  transfers between devices with their start and end apart: 40 -> 49, of which waited for: 19 -> 19; matrix products, arithmetic and copies ran while one was open for 15% -> 12% of each run, Pallas kernels for 7% -> 20%
where the time goes in v2:
time: 422 us; the launch traced here: 419 us
  Pallas kernels  117 us (28%)
  starting transfers between devices  103 us (24%)
  waiting for transfers between devices  91 us (22%)
  local copies, waits for them, and re-layouts  45.6 us (11%)
  other arithmetic  26.8 us (6%)
  matrix products  19.7 us (5%)
  between operations  16.5 us (4%)
    all_to_all x6, starting transfers between devices, exchange(): lax.all_to_all(blocks, 'ctx', 0, 0, tiled=True, axis_index_groups=teams)  49.3 us
    pallas_call x2, Pallas kernels, attention_backward(): pl.pallas_call(functools.partial(backward_kernel, pair_at, first_chunk, p...  49 us
    all_to_all x6, waiting for transfers between devices, exchange(): lax.all_to_all(blocks, 'ctx', 0, 0, tiled=True, axis_index_groups=teams)  39.6 us
    ppermute x4, waiting for transfers between devices, halved(): lax.ppermute(sent, 'ctx', [(i, i ^ 1 << bit) for i in range(cycle_size)])  34.7 us
    pallas_call x1, Pallas kernels, middle_part(): pl.pallas_call(middle_kernel, grid=(wide // tile,), out_shape=tuple((jax....  33.8 us
    pallas_call x2, Pallas kernels, attention_forward(): pl.pallas_call(functools.partial(forward_kernel, pair_at, first_chunk, pe...  33.8 us
    ppermute x24, starting transfers between devices, exchange(): lax.ppermute(array, 'ctx', [(i, i ^ 1 << bit) for i in range(cycle_size)])  31.4 us
    unnamed x164, local copies, waits for them, and re-layouts  23.5 us
  transfers between devices with their start and end apart: 49, of which 19 were waited for; matrix products, arithmetic and copies ran while one was open for 12% of the time, Pallas kernels for 20%

profile of v2, /device:TPU:0, one launch (start us, length us, event | category | flops | bytes accessed | tf_op | source)
XLA Modules:
  0.0 419.0 jit_solution(8302383098746977456)
XLA Ops:
  31.5 8.4 %all-to-all-start = ((bf16[16,192,256]{2,1,0:T(8,128)(2,1)}), bf16[16,192,256]{2,1,0:T(8,128)(2,1)S(1)}, u32[]{:S(2)}, u32[]{:S(2)}) async-start(bf16[16,192,256]{2,1,0:T(8,128)(2,1)} %pad_maximum_fusion), calls=%async_computation | async-start | bytes 3145728 | tf_op jit(solution)/shard_map/all_to_all | solution.py:568
  40.7 33.5 %all-to-all-done.query_ref.own_ref = bf16[16,192,256]{2,1,0:T(8,128)(2,1)S(1)} async-done(((bf16[16,192,256]{2,1,0:T(8,128)(2,1)}), bf16[16,192,256]{2,1,0:T(8,128)(2,1)S(1)}, u32[]{:S(2)}, u32[]{:S(2)}) %all-to-all-start) | async-done | bytes 1572896 | tf_op jit(solution)/shard_map/all_to_all | solution.py:568
  76.3 8.0 %all-to-all-start.1 = ((bf16[16,128,256]{2,1,0:T(8,128)(2,1)}), bf16[16,128,256]{2,1,0:T(8,128)(2,1)}, u32[]{:S(2)}, u32[]{:S(2)}) async-start(bf16[16,128,256]{2,1,0:T(8,128)(2,1)} %broadcast_in_dim.45), calls=%async_computation.1 | async-start | bytes 2097152 | tf_op jit(solution)/shard_map/all_to_all | solution.py:568
  84.3 31.6 %attention_forward.1 = (bf16[16,64,256]{2,1,0:T(8,128)(2,1)}, f32[8,64,512]{2,1,0:T(8,128)S(1)}, f32[8,1,512]{2,1,0:T(1,128)S(1)}, bf16[8192,128]{1,0:T(8,128)(2,1)}) custom-call(s32[8,7]{1,0:T(8,128)S(1)} %stack.36.meta_ref, s32[8,1,512]{2,1,0:T(1,128)S(1)} %reshape.306.starts_ref, bf16[16,192,256]{2,1,0:T(8,128)(2,1)S(1)} %all-to-all-done.query_ref.own_ref, ...), custom_call_target="tpu_custom_call" | custom-call | flops 30000001024 | bytes 30000000 | tf_op jit(solution)/shard_map/attention_forward/pallas_call | solution.py:190
  118.1 6.9 %all-to-all-start.2 = ((bf16[16,64,256]{2,1,0:T(8,128)(2,1)}), bf16[16,64,256]{2,1,0:T(8,128)(2,1)}, u32[]{:S(2)}, u32[]{:S(2)}) async-start(bf16[16,64,256]{2,1,0:T(8,128)(2,1)} %get-tuple-element.47), calls=%async_computation.2 | async-start | bytes 1048576 | tf_op jit(solution)/shard_map/all_to_all | solution.py:568
  134.3 6.1 %all-to-all-done.2 = bf16[16,64,256]{2,1,0:T(8,128)(2,1)} async-done(((bf16[16,64,256]{2,1,0:T(8,128)(2,1)}), bf16[16,64,256]{2,1,0:T(8,128)(2,1)}, u32[]{:S(2)}, u32[]{:S(2)}) %all-to-all-start.2) | async-done | bytes 524320 | tf_op jit(solution)/shard_map/all_to_all | solution.py:568
  142.5 33.8 %middle_part.1 = (bf16[1088,256]{1,0:T(8,128)(2,1)}, f32[1088,256]{1,0:T(8,128)S(1)}, bf16[1088,256]{1,0:T(8,128)(2,1)S(1)}, bf16[13056,128]{1,0:T(8,128)(2,1)}) custom-call(s32[1]{0:T(128)} %bitcast.core_ref, bf16[1088,256]{1,0:T(8,128)(2,1)S(1)} %bitcast.111, bf16[1088,256]{1,0:T(8,128)(2,1)S(1)} %bitcast.109, bf16[1088,256]{1,0:T(8,128)(2,1)S(1)} %bitcast.112, ...), custom_call_target="tpu_custom_call" | custom-call | flops 1000000000 | bytes 1000000 | tf_op jit(solution)/shard_map/middle_part/pallas_call | solution.py:386
  176.3 3.1 constant_dynamic-slice_fusion.16
  183.5 6.1 %last_backward.1 = (bf16[1,64,256]{2,1,0:T(8,128)(2,1)S(1)}, f32[16,128,256]{2,1,0:T(8,128)S(1)}, bf16[16,128,256]{2,1,0:T(8,128)(2,1)}) custom-call(s32[1,7]{1,0:T(1,128)S(1)} %copy-done.18, s32[1,1,256]{2,1,0:T(1,128)S(1)} %bitcast.121, bf16[1,64,256]{2,1,0:T(8,128)(2,1)S(1)} %slice_bitcast_fusion.6.query_ref, ...), custom_call_target="tpu_custom_call" | custom-call | flops 6000000000 | bytes 6000000 | tf_op jit(solution)/shard_map/last_backward/pallas_call | solution.py:211
  196.0 9.4 %all-to-all-start.3 = ((bf16[16,64,256]{2,1,0:T(8,128)(2,1)}), bf16[16,64,256]{2,1,0:T(8,128)(2,1)S(1)}, u32[]{:S(2)}, u32[]{:S(2)}) async-start(bf16[16,64,256]{2,1,0:T(8,128)(2,1)} %bitcast.130), calls=%async_computation.3 | async-start | bytes 1048576 | tf_op jit(solution)/shard_map/all_to_all | solution.py:568
  205.4 2.6 add_convert_fusion.1
  208.0 11.3 %collective-permute-done.11 = bf16[3264,128]{1,0:T(8,128)(2,1)} collective-permute-done((bf16[3264,128]{1,0:T(8,128)(2,1)}, bf16[3264,128]{1,0:T(8,128)(2,1)}, u32[]{:S(2)}, u32[]{:S(2)}) %collective-permute-start.11) | collective-permute-done | bytes 835616 | tf_op jit(solution)/shard_map/ppermute | solution.py:459
  221.7 9.7 %all-to-all-start.4 = ((bf16[16,128,256]{2,1,0:T(8,128)(2,1)}), bf16[16,128,256]{2,1,0:T(8,128)(2,1)}, u32[]{:S(2)}, u32[]{:S(2)}) async-start(bf16[16,128,256]{2,1,0:T(8,128)(2,1)} %add_convert_fusion.1), calls=%async_computation.4 | async-start | bytes 2097152 | tf_op jit(solution)/shard_map/all_to_all | solution.py:568
  232.6 43.0 %attention_backward.1 = (bf16[16,64,256]{2,1,0:T(8,128)(2,1)S(1)}, f32[16,128,256]{2,1,0:T(8,128)}, bf16[16,128,256]{2,1,0:T(8,128)(2,1)S(1)}) custom-call(s32[8,7]{1,0:T(8,128)S(1)} %copy-done.14, s32[8,1,512]{2,1,0:T(1,128)S(1)} %copy-done.12, bf16[16,192,256]{2,1,0:T(8,128)(2,1)S(1)} %copy-done.3, bf16[16,192,256]{2,1,0:T(8,128)(2,1)S(1)} %copy-done.3, ...), custom_call_target="tpu_custom_call" | custom-call | flops 40000000000 | bytes 40000000 | tf_op jit(solution)/shard_map/attention_backward/pallas_call | solution.py:211
  275.6 2.7 collective-permute-done.12
  281.4 7.0 %all-to-all-start.5 = ((bf16[16,192,256]{2,1,0:T(8,128)(2,1)}), bf16[16,192,256]{2,1,0:T(8,128)(2,1)S(1)}, u32[]{:S(2)}, u32[]{:S(2)}) async-start(bf16[16,192,256]{2,1,0:T(8,128)(2,1)} %pad_maximum_fusion.1), calls=%async_computation.5 | async-start | bytes 3145728 | tf_op jit(solution)/shard_map/all_to_all | solution.py:568
  288.4 9.8 %all-gather.3.cloned.1.call-start = ((), (), s32[]{:S(2)}) async-start(), calls=%async_computation.6 | async-start | bytes 3446784 | tf_op jit(solution)/shard_map/all_gather | solution.py:654
  300.9 15.1 %collective-permute-done.39 = bf16[1632,128]{1,0:T(8,128)(2,1)} collective-permute-done((bf16[1632,128]{1,0:T(8,128)(2,1)}, bf16[1632,128]{1,0:T(8,128)(2,1)}, u32[]{:S(2)}, u32[]{:S(2)}) %collective-permute-start.39) | collective-permute-done | bytes 417824 | tf_op jit(solution)/shard_map/ppermute | solution.py:459
  317.9 4.5 %collective-permute-start.40 = (bf16[816,128]{1,0:T(8,128)(2,1)S(1)}, bf16[816,128]{1,0:T(8,128)(2,1)S(1)}, u32[]{:S(2)}, u32[]{:S(2)}) collective-permute-start(bf16[816,128]{1,0:T(8,128)(2,1)S(1)} %constant_dynamic-slice_fusion.1), channel_id=1, source_target_pairs={{0,8},{2,10},{4,12},{6,14},{8,0},{10,2},{12,4},{14,6},{16,24},{18,... | collective-permute-start | bytes 626696 | tf_op jit(solution)/shard_map/ppermute | solution.py:459
  323.8 3.5 collective-permute-done.40
  330.1 4.7 %collective-permute-done.41 = bf16[408,128]{1,0:T(8,128)(2,1)S(1)} collective-permute-done((bf16[408,128]{1,0:T(8,128)(2,1)S(1)}, bf16[408,128]{1,0:T(8,128)(2,1)S(1)}, u32[]{:S(2)}, u32[]{:S(2)}) %collective-permute-start.41) | collective-permute-done | bytes 104480 | tf_op jit(solution)/shard_map/ppermute | solution.py:459
  354.8 3.1 collective-permute-done.30
  392.6 3.8 collective-permute-done.37
  400.5 2.5 convert_multiply_fusion
  (405 shorter events, 132.4 us)
Async XLA Ops:
  10.5 13.7 %collective-permute-start.3 = (bf16[544,1088]{1,0:T(8,128)(2,1)}, bf16[544,1088]{1,0:T(8,128)(2,1)}, u32[]{:S(2)}, u32[]{:S(2)}) collective-permute-start(bf16[544,1088]{1,0:T(8,128)(2,1)} %param.35), channel_id=1, source_target_pairs={{0,1},{1,0},{2,3},{3,2},{4,5},{5,4},{6,7},{7,6},{8,9},{9,8},{10,11... | collective-permute-start | bytes 3551240 | tf_op jit(solution)/shard_map/ppermute | solution.py:547
  10.6 11.2 %collective-permute-start.2 = (bf16[544,1088]{1,0:T(8,128)(2,1)}, bf16[544,1088]{1,0:T(8,128)(2,1)}, u32[]{:S(2)}, u32[]{:S(2)}) collective-permute-start(bf16[544,1088]{1,0:T(8,128)(2,1)} %param.34), channel_id=1, source_target_pairs={{0,1},{1,0},{2,3},{3,2},{4,5},{5,4},{6,7},{7,6},{8,9},{9,8},{10,11... | collective-permute-start | bytes 3551240 | tf_op jit(solution)/shard_map/ppermute | solution.py:547
  11.0 15.8 %collective-permute-start.1 = (bf16[544,1088]{1,0:T(8,128)(2,1)}, bf16[544,1088]{1,0:T(8,128)(2,1)S(1)}, u32[]{:S(2)}, u32[]{:S(2)}) collective-permute-start(bf16[544,1088]{1,0:T(8,128)(2,1)} %param.33), channel_id=1, source_target_pairs={{0,1},{1,0},{2,3},{3,2},{4,5},{5,4},{6,7},{7,6},{8,9},{9,8},{10,11... | collective-permute-start | bytes 3551240 | tf_op jit(solution)/shard_map/ppermute | solution.py:547
  31.5 42.7 %all-to-all-start = ((bf16[16,192,256]{2,1,0:T(8,128)(2,1)}), bf16[16,192,256]{2,1,0:T(8,128)(2,1)S(1)}, u32[]{:S(2)}, u32[]{:S(2)}) async-start(bf16[16,192,256]{2,1,0:T(8,128)(2,1)} %pad_maximum_fusion), calls=%async_computation | async-start | bytes 3145728 | tf_op jit(solution)/shard_map/all_to_all | solution.py:568
  74.2 10.1 %collective-permute-start.4 = (bf16[16,192,256]{2,1,0:T(8,128)(2,1)S(1)}, bf16[16,192,256]{2,1,0:T(8,128)(2,1)}, u32[]{:S(2)}, u32[]{:S(2)}) collective-permute-start(bf16[16,192,256]{2,1,0:T(8,128)(2,1)S(1)} %all-to-all-done.query_ref.own_ref), channel_id=1, source_target_pairs={{0,1},{1,0},{2,3},{3,2},{4,5},{5,4},{6,7},{7,6},{8,9},{9,8},{10,11... | collective-permute-start | bytes 4718600 | tf_op jit(solution)/shard_map/ppermute | solution.py:547
  74.2 67.2 %collective-permute-start.8 = (bf16[544,4352]{1,0:T(8,128)(2,1)}, bf16[544,4352]{1,0:T(8,128)(2,1)}, u32[]{:S(2)}, u32[]{:S(2)}) collective-permute-start(bf16[544,4352]{1,0:T(8,128)(2,1)} %bitcast.125), channel_id=1, source_target_pairs={{0,1},{1,0},{2,3},{3,2},{4,5},{5,4},{6,7},{7,6},{8,9},{9,8},{10,11... | collective-permute-start | bytes 14204936 | tf_op jit(solution)/shard_map/ppermute | solution.py:547
  74.7 66.7 %collective-permute-start.7 = (bf16[544,4352]{1,0:T(8,128)(2,1)}, bf16[544,4352]{1,0:T(8,128)(2,1)}, u32[]{:S(2)}, u32[]{:S(2)}) collective-permute-start(bf16[544,4352]{1,0:T(8,128)(2,1)} %up_own_ref.1), channel_id=1, source_target_pairs={{0,1},{1,0},{2,3},{3,2},{4,5},{5,4},{6,7},{7,6},{8,9},{9,8},{10,11... | collective-permute-start | bytes 14204936 | tf_op jit(solution)/shard_map/ppermute | solution.py:547
  76.3 41.3 %all-to-all-start.1 = ((bf16[16,128,256]{2,1,0:T(8,128)(2,1)}), bf16[16,128,256]{2,1,0:T(8,128)(2,1)}, u32[]{:S(2)}, u32[]{:S(2)}) async-start(bf16[16,128,256]{2,1,0:T(8,128)(2,1)} %broadcast_in_dim.45), calls=%async_computation.1 | async-start | bytes 2097152 | tf_op jit(solution)/shard_map/all_to_all | solution.py:568
  117.6 9.7 %collective-permute-start.5 = (bf16[16,128,256]{2,1,0:T(8,128)(2,1)}, bf16[16,128,256]{2,1,0:T(8,128)(2,1)S(1)}, u32[]{:S(2)}, u32[]{:S(2)}) collective-permute-start(bf16[16,128,256]{2,1,0:T(8,128)(2,1)} %all-to-all-done.1.own_ref), channel_id=1, source_target_pairs={{0,1},{1,0},{2,3},{3,2},{4,5},{5,4},{6,7},{7,6},{8,9},{9,8},{10,11... | collective-permute-start | bytes 3145736 | tf_op jit(solution)/shard_map/ppermute | solution.py:547
  117.8 23.6 %collective-permute-start.6 = (bf16[544,1088]{1,0:T(8,128)(2,1)}, bf16[544,1088]{1,0:T(8,128)(2,1)}, u32[]{:S(2)}, u32[]{:S(2)}) collective-permute-start(bf16[544,1088]{1,0:T(8,128)(2,1)} %out_own_ref.1), channel_id=1, source_target_pairs={{0,1},{1,0},{2,3},{3,2},{4,5},{5,4},{6,7},{7,6},{8,9},{9,8},{10,11... | collective-permute-start | bytes 3551240 | tf_op jit(solution)/shard_map/ppermute | solution.py:547
  118.1 22.2 %all-to-all-start.2 = ((bf16[16,64,256]{2,1,0:T(8,128)(2,1)}), bf16[16,64,256]{2,1,0:T(8,128)(2,1)}, u32[]{:S(2)}, u32[]{:S(2)}) async-start(bf16[16,64,256]{2,1,0:T(8,128)(2,1)} %get-tuple-element.47), calls=%async_computation.2 | async-start | bytes 1048576 | tf_op jit(solution)/shard_map/all_to_all | solution.py:568
  179.5 10.6 %collective-permute-start.10 = (bf16[6528,128]{1,0:T(8,128)(2,1)}, bf16[6528,128]{1,0:T(8,128)(2,1)}, u32[]{:S(2)}, u32[]{:S(2)}) collective-permute-start(bf16[6528,128]{1,0:T(8,128)(2,1)} %constant_dynamic-slice_fusion.16), channel_id=1, source_target_pairs={{0,1},{1,0},{2,3},{3,2},{4,5},{5,4},{6,7},{7,6},{8,9},{9,8},{10,11... | collective-permute-start | bytes 5013512 | tf_op jit(solution)/shard_map/ppermute | solution.py:547
  189.6 15.8 %collective-permute-start.9 = (bf16[16,128,256]{2,1,0:T(8,128)(2,1)}, bf16[16,128,256]{2,1,0:T(8,128)(2,1)}, u32[]{:S(2)}, u32[]{:S(2)}) collective-permute-start(bf16[16,128,256]{2,1,0:T(8,128)(2,1)} %get-tuple-element.58), channel_id=1, source_target_pairs={{0,1},{1,0},{2,3},{3,2},{4,5},{5,4},{6,7},{7,6},{8,9},{9,8},{10,11... | collective-permute-start | bytes 3145736 | tf_op jit(solution)/shard_map/ppermute | solution.py:547
  194.1 25.2 %collective-permute-start.11 = (bf16[3264,128]{1,0:T(8,128)(2,1)}, bf16[3264,128]{1,0:T(8,128)(2,1)}, u32[]{:S(2)}, u32[]{:S(2)}) collective-permute-start(bf16[3264,128]{1,0:T(8,128)(2,1)} %constant_dynamic-slice_fusion.15), channel_id=1, source_target_pairs={{0,2},{2,0},{4,6},{6,4},{8,10},{10,8},{12,14},{14,12},{16,18},{18,... | collective-permute-start | bytes 2506760 | tf_op jit(solution)/shard_map/ppermute | solution.py:459
  196.0 25.6 %all-to-all-start.3 = ((bf16[16,64,256]{2,1,0:T(8,128)(2,1)}), bf16[16,64,256]{2,1,0:T(8,128)(2,1)S(1)}, u32[]{:S(2)}, u32[]{:S(2)}) async-start(bf16[16,64,256]{2,1,0:T(8,128)(2,1)} %bitcast.130), calls=%async_computation.3 | async-start | bytes 1048576 | tf_op jit(solution)/shard_map/all_to_all | solution.py:568
  221.7 58.5 %all-to-all-start.4 = ((bf16[16,128,256]{2,1,0:T(8,128)(2,1)}), bf16[16,128,256]{2,1,0:T(8,128)(2,1)}, u32[]{:S(2)}, u32[]{:S(2)}) async-start(bf16[16,128,256]{2,1,0:T(8,128)(2,1)} %add_convert_fusion.1), calls=%async_computation.4 | async-start | bytes 2097152 | tf_op jit(solution)/shard_map/all_to_all | solution.py:568
  281.4 54.0 %all-to-all-start.5 = ((bf16[16,192,256]{2,1,0:T(8,128)(2,1)}), bf16[16,192,256]{2,1,0:T(8,128)(2,1)S(1)}, u32[]{:S(2)}, u32[]{:S(2)}) async-start(bf16[16,192,256]{2,1,0:T(8,128)(2,1)} %pad_maximum_fusion.1), calls=%async_computation.5 | async-start | bytes 3145728 | tf_op jit(solution)/shard_map/all_to_all | solution.py:568
  288.4 112.1 %all-gather.3.cloned.1.call-start = ((), (), s32[]{:S(2)}) async-start(), calls=%async_computation.6 | async-start | bytes 3446784 | tf_op jit(solution)/shard_map/all_gather | solution.py:654
  299.0 17.0 %collective-permute-start.39 = (bf16[1632,128]{1,0:T(8,128)(2,1)}, bf16[1632,128]{1,0:T(8,128)(2,1)}, u32[]{:S(2)}, u32[]{:S(2)}) collective-permute-start(bf16[1632,128]{1,0:T(8,128)(2,1)} %constant_dynamic-slice_fusion.2), channel_id=1, source_target_pairs={{0,4},{2,6},{4,0},{6,2},{8,12},{10,14},{12,8},{14,10},{16,20},{18,... | collective-permute-start | bytes 1253384 | tf_op jit(solution)/shard_map/ppermute | solution.py:459
  317.9 9.4 %collective-permute-start.40 = (bf16[816,128]{1,0:T(8,128)(2,1)S(1)}, bf16[816,128]{1,0:T(8,128)(2,1)S(1)}, u32[]{:S(2)}, u32[]{:S(2)}) collective-permute-start(bf16[816,128]{1,0:T(8,128)(2,1)S(1)} %constant_dynamic-slice_fusion.1), channel_id=1, source_target_pairs={{0,8},{2,10},{4,12},{6,14},{8,0},{10,2},{12,4},{14,6},{16,24},{18,... | collective-permute-start | bytes 626696 | tf_op jit(solution)/shard_map/ppermute | solution.py:459
  327.5 7.3 %collective-permute-start.41 = (bf16[408,128]{1,0:T(8,128)(2,1)S(1)}, bf16[408,128]{1,0:T(8,128)(2,1)S(1)}, u32[]{:S(2)}, u32[]{:S(2)}) collective-permute-start(bf16[408,128]{1,0:T(8,128)(2,1)S(1)} %constant_dynamic-slice_fusion), channel_id=1, source_target_pairs={{0,16},{2,18},{4,20},{6,22},{8,24},{10,26},{12,28},{14,30},{16,0},... | collective-permute-start | bytes 313352 | tf_op jit(solution)/shard_map/ppermute | solution.py:459
  342.0 9.8 %collective-permute-start.13 = (bf16[3456,128]{1,0:T(8,128)(2,1)S(1)}, bf16[3456,128]{1,0:T(8,128)(2,1)S(1)}, u32[]{:S(2)}, u32[]{:S(2)}) collective-permute-start(bf16[3456,128]{1,0:T(8,128)(2,1)S(1)} %pad_dynamic-slice_fusion), channel_id=1, source_target_pairs={{0,1},{1,0},{2,3},{3,2},{4,5},{5,4},{6,7},{7,6},{8,9},{9,8},{10,11... | collective-permute-start | bytes 2654216 | tf_op jit(solution)/shard_map/ppermute | solution.py:434
  352.5 7.0 %collective-permute-start.22 = (bf16[576,128]{1,0:T(8,128)(2,1)S(1)}, bf16[576,128]{1,0:T(8,128)(2,1)S(1)}, u32[]{:S(2)}, u32[]{:S(2)}) collective-permute-start(bf16[576,128]{1,0:T(8,128)(2,1)S(1)} %constant_dynamic-slice_fusion.10), channel_id=1, source_target_pairs={{0,4},{2,6},{4,0},{6,2},{8,12},{10,14},{12,8},{14,10},{16,20},{18,... | collective-permute-start | bytes 442376 | tf_op jit(solution)/shard_map/ppermute | solution.py:431
  388.2 8.2 %collective-permute-start.37 = (bf16[576,128]{1,0:T(8,128)(2,1)S(1)}, bf16[576,128]{1,0:T(8,128)(2,1)S(1)}, u32[]{:S(2)}, u32[]{:S(2)}) collective-permute-start(bf16[576,128]{1,0:T(8,128)(2,1)S(1)} %constant_dynamic-update-slice_fusion.8), channel_id=1, source_target_pairs={{0,8},{2,10},{4,12},{6,14},{8,0},{10,2},{12,4},{14,6},{16,24},{18,... | collective-permute-start | bytes 442376 | tf_op jit(solution)/shard_map/ppermute | solution.py:431
  (106 other events, 654.9 us)
Sparse Core Ops, SparseCore 0:
  335.6 62.3 all-gather.2
